TPU v7x, 256 devices: a whole 4x4x8 slice. The times are simulated.
256 devices in a mesh: walkers: 4 (over x_hi, core), band: 64 (over z, y, x_lo).
Axes of the slice: x: 4 (x_hi: 2, x_lo: 2; x = x_hi * 2 + x_lo), y: 4, z: 8, core: 2. Of those that a mesh axis runs over, the one named last changes fastest.
Arguments:
- orbitals: bfloat16 [256, 2048, 128], P(('walkers', 'band')), parts along dimension 0, may hold values from -6 to 6
Outputs:
- exchange: float32 [256, 2048, 128], P(('walkers', 'band')), parts along dimension 0
There are 4 independent parts, one for each index of `walkers`. A program takes and returns all parts, laid end to end along the dimension named above; each array names one. Nothing has to cross between parts.
All inputs are finite; a program needn't handle non-finite values.
Results may differ from a plain program's by a relative error of at most 0.005.
The roundings to bfloat16 on the way count: a program that leaves them out, or rounds other values in their place, can miss the bound.
Values may be sent and summed in bfloat16 or wider, within the bound.
No kernel may reach another device: no remote copies, remote signals or barrier semaphores. Data moves between devices by JAX's collectives and lax.ppermute only.
A program may use at most 64 MiB of HBM per device.

v0:
```python
import functools
import math

import jax
import jax.numpy as jnp
import ml_dtypes
import numpy as np
from jax import lax
from jax.experimental import pallas as pl
from jax.experimental.pallas import tpu as pltpu
from jax.sharding import PartitionSpec as P

NG = 64
HALF = 32
LANES = 128
SLOTS = 4
MIXING = 0.25


def dft_tables():
    index_row = np.arange(NG)
    angle = (index_row[:, None] * index_row[None, :] % NG).astype(np.float32)
    angle = angle * np.float32(2.0 * math.pi / NG)
    return [f(angle).astype(ml_dtypes.bfloat16).astype(np.float32) for f in (np.cos, np.sin)]


def paired(table_cos, table_sin, sign):
    return np.block([[table_cos, sign * table_sin], [-sign * table_sin, table_cos]])


def make_tables():
    cosine, sine = dft_tables()
    into = np.zeros((SLOTS, 2, NG, 2, 2, SLOTS, HALF), np.float32)
    back = np.zeros((2, 2, SLOTS, HALF, SLOTS, 2, NG), np.float32)
    for band in range(SLOTS):
        even = band - band % 2
        for parity in range(2):
            into[band, parity, :, parity, 0, band, 1:] = cosine[:, 1:HALF]
            into[band, parity, :, parity, 1, band, 1:] = -sine[:, 1:HALF]
            back[parity, 0, band, 1:, band, parity, :] = 2 * cosine[1:HALF]
            back[parity, 1, band, 1:, band, parity, :] = -2 * sine[1:HALF]
            for place, plane in ((even, 0), (even + 1, HALF)):
                into[band, parity, :, parity, band % 2, place, 0] = cosine[:, plane]
                back[parity, band % 2, place, 0, band, parity, :] = cosine[plane]
    into = into.reshape(SLOTS * LANES, SLOTS * LANES)
    back = back.reshape(SLOTS * LANES, SLOTS * LANES)
    order = np.arange(NG).reshape(HALF, 2).T
    y_in = np.concatenate([np.concatenate([order[b] + NG * c for c in range(2)]) for b in range(2)])
    forward = paired(cosine, sine, 1.0)
    inverse = paired(cosine, sine, -1.0)
    wave = np.arange(NG)
    wave = np.where(wave < HALF, wave, wave - NG)
    slots = np.tile(np.arange(HALF), (SLOTS, 1))
    slots[1::2, 0] = HALF
    squared = wave[:, None, None] ** 2 + wave[None, :, None] ** 2 + slots.reshape(-1)[None, None, :] ** 2
    strength = np.float32(NG**1.5 / 4.0)
    kernel = np.where(squared > 0, strength / np.maximum(squared, 1).astype(np.float32), np.float32(0))
    as_bf = lambda table: table.astype(ml_dtypes.bfloat16)
    return (
        as_bf(into),
        as_bf(forward[:, y_in]),
        as_bf(forward),
        kernel.reshape(NG * NG, LANES).astype(np.float32),
        as_bf(inverse),
        as_bf(inverse[y_in]),
        as_bf(back),
    )


def dot(left, right):
    return jnp.dot(left, right, preferred_element_type=jnp.float32)


def exchange_kernel(steps, own_ref, ahead_ref, behind_ref, *refs):
    into, y_fwd, x_fwd, kernel, x_inv, y_inv, back, out_ref, to_ahead, to_behind, planes, flat, spec = refs
    block, x_unroll = steps
    rows = block * HALF

    def wide(ref, base):
        return ref[pl.ds(base, rows), :].astype(jnp.float32)

    @pl.loop(0, NG // block)
    def _(at):
        base = pl.multiple_of(at * rows, rows)
        own, ahead, behind = (wide(ref, base) for ref in (own_ref, ahead_ref, behind_ref))
        density = [own * own, own * ahead, behind * own, behind * ahead]
        density = jnp.concatenate([d.astype(jnp.bfloat16) for d in density], axis=1)
        flat[...] = dot(density, into[...]).astype(jnp.bfloat16)
        for pair in range(block // 2):
            section = []
            for x in (2 * pair, 2 * pair + 1):
                section.append(
                    jnp.concatenate(
                        [flat[x * HALF : (x + 1) * HALF, t * LANES : (t + 1) * LANES] for t in range(4)], axis=0
                    )
                )
            second = dot(y_fwd[...], jnp.concatenate(section, axis=1))
            for n in range(2):
                place = pl.multiple_of((at * block + 2 * pair + n) * LANES, LANES)
                planes[pl.ds(place, LANES), :] = second[:, n * LANES : (n + 1) * LANES]

    @pl.loop(0, NG // (2 * x_unroll))
    def _(at):
        for pair in range(x_unroll):
            ky = (at * x_unroll + pair) * 2
            section = jnp.concatenate(
                [
                    jnp.concatenate(
                        [planes[pl.ds(ky + n + c * NG, NG, stride=LANES), :] for c in range(2)], axis=0
                    ).astype(jnp.bfloat16)
                    for n in range(2)
                ],
                axis=1,
            )
            spectrum = dot(x_fwd[...], section)
            weight = jnp.concatenate(
                [kernel[pl.ds(pl.multiple_of((ky + n) * NG, NG), NG), :] for n in range(2)], axis=1
            )
            weight = jnp.concatenate([weight, weight], axis=0)
            spectrum = (spectrum * weight).astype(jnp.bfloat16)
            back_one = dot(x_inv[...], spectrum)
            for n in range(2):
                place = pl.multiple_of((ky + n) * LANES, LANES)
                spec[pl.ds(place, LANES), :] = back_one[:, n * LANES : (n + 1) * LANES]

    @pl.loop(0, NG // block)
    def _(at):
        for pair in range(block // 2):
            x = at * block + 2 * pair
            section = jnp.concatenate(
                [
                    jnp.concatenate(
                        [spec[pl.ds(x + n + c * NG, NG, stride=LANES), :] for c in range(2)], axis=0
                    ).astype(jnp.bfloat16)
                    for n in range(2)
                ],
                axis=1,
            )
            back_two = dot(y_inv[...], section).astype(jnp.bfloat16)
            for n in range(2):
                row = (2 * pair + n) * HALF
                for t in range(4):
                    flat[row : row + HALF, t * LANES : (t + 1) * LANES] = back_two[
                        t * HALF : (t + 1) * HALF, n * LANES : (n + 1) * LANES
                    ]
        base = pl.multiple_of(at * rows, rows)
        field = dot(flat[...], back[...]) * (-MIXING / NG**3)
        alone, onward, rearward, across = (field[:, p * LANES : (p + 1) * LANES] for p in range(SLOTS))
        own, ahead, behind = (wide(ref, base) for ref in (own_ref, ahead_ref, behind_ref))
        out_ref[pl.ds(base, rows), :] = own * alone + ahead * onward + behind * rearward
        to_ahead[pl.ds(base, rows), :] = (own * onward + behind * across).astype(jnp.bfloat16)
        to_behind[pl.ds(base, rows), :] = (own * rearward + ahead * across).astype(jnp.bfloat16)


def exchange(own, ahead, behind, steps=(32, 16)):
    tables = [jnp.asarray(t) for t in make_tables()]
    operands = [own, ahead, behind, *tables]
    block = pl.BlockSpec(memory_space=pltpu.VMEM)
    return pl.pallas_call(
        functools.partial(exchange_kernel, steps),
        out_shape=[jax.ShapeDtypeStruct(own.shape, t) for t in (jnp.float32, jnp.bfloat16, jnp.bfloat16)],
        in_specs=[block] * len(operands),
        out_specs=[block] * 3,
        scratch_shapes=[
            pltpu.VMEM((NG * LANES, LANES), jnp.float32),
            pltpu.VMEM((steps[0] * HALF, SLOTS * LANES), jnp.bfloat16),
            pltpu.VMEM((NG * LANES, LANES), jnp.float32),
        ],
        compiler_params=pltpu.CompilerParams(vmem_limit_bytes=48 * 1024 * 1024),
        cost_estimate=pl.CostEstimate(flops=2**32, bytes_accessed=8 << 20, transcendentals=0),
    )(*operands)


def shifted(x, by):
    count = lax.axis_size("band")
    return lax.ppermute(x, "band", [(i, (i + by) % count) for i in range(count)])


def local(orbitals):
    own = orbitals[0]
    behind = shifted(own, 1)
    ahead = shifted(own, -2)
    total, to_ahead, to_behind = exchange(own, ahead, behind)
    total = total + shifted(to_behind, -1).astype(jnp.float32)
    total = total + shifted(to_ahead, 2).astype(jnp.float32)
    return total[None]


def solution(mesh):
    return jax.shard_map(
        local,
        mesh=mesh,
        in_specs=(P(("walkers", "band"), None, None),),
        out_specs=P(("walkers", "band"), None, None),
        check_vma=False,
    )
```

profile of v0, /device:TPU:4, one launch (start us, length us, event | category | flops | bytes accessed | tf_op | source)
XLA Modules:
  0.0 60.1 jit_solution(11338991164042832708)
XLA Ops:
  0.0 1.2 %collective-permute-start.1 = (bf16[2048,128]{1,0:T(8,128)(2,1)}, bf16[2048,128]{1,0:T(8,128)(2,1)S(1)}, u32[]{:S(2)}, u32[]{:S(2)}) collective-permute-start(bf16[2048,128]{1,0:T(8,128)(2,1)} %bitcast.3), channel_id=1, source_target_pairs={{0,1},{1,2},{2,3},{3,4},{4,5},{5,6},{6,7},{7,8},{8,9},{9,10},{10,1... | collective-permute-start | bytes 1572872 | tf_op jit(solution)/shard_map/ppermute | solution.py:176
  1.2 8.3 %collective-permute-start = (bf16[2048,128]{1,0:T(8,128)(2,1)}, bf16[2048,128]{1,0:T(8,128)(2,1)S(1)}, u32[]{:S(2)}, u32[]{:S(2)}) collective-permute-start(bf16[2048,128]{1,0:T(8,128)(2,1)} %bitcast.4), channel_id=1, source_target_pairs={{0,62},{1,63},{2,0},{3,1},{4,2},{5,3},{6,4},{7,5},{8,6},{9,7},{10,... | collective-permute-start | bytes 1572872 | tf_op jit(solution)/shard_map/ppermute | solution.py:176
  9.5 11.6 %collective-permute-done.1.behind_ref = bf16[2048,128]{1,0:T(8,128)(2,1)S(1)} collective-permute-done((bf16[2048,128]{1,0:T(8,128)(2,1)}, bf16[2048,128]{1,0:T(8,128)(2,1)S(1)}, u32[]{:S(2)}, u32[]{:S(2)}) %collective-permute-start.1) | collective-permute-done | bytes 524320 | tf_op jit(solution)/shard_map/ppermute | solution.py:176
  21.1 0.0 collective-permute-done.ahead_ref
  21.1 0.0 copy-start
  21.1 1.0 %copy-done = bf16[1,2048,128]{2,1,0:T(8,128)(2,1)S(1)} copy-done((bf16[1,2048,128]{2,1,0:T(8,128)(2,1)S(1)}, bf16[1,2048,128]{2,1,0:T(8,128)(2,1)}, u32[]{:S(2)}) %copy-start) | copy-done | bytes 524312
  22.1 0.0 copy-start.1
  22.1 1.0 %copy-done.1 = bf16[512,512]{1,0:T(8,128)(2,1)S(1)} copy-done((bf16[512,512]{1,0:T(8,128)(2,1)S(1)}, bf16[512,512]{1,0:T(8,128)(2,1)}, u32[]{:S(2)}) %copy-start.1) | copy-done | bytes 524312
  23.2 0.0 copy-start.2
  23.2 1.0 %copy-done.2 = bf16[512,512]{1,0:T(8,128)(2,1)S(1)} copy-done((bf16[512,512]{1,0:T(8,128)(2,1)S(1)}, bf16[512,512]{1,0:T(8,128)(2,1)}, u32[]{:S(2)}) %copy-start.2) | copy-done | bytes 524312
  24.2 0.0 copy-start.3
  24.2 0.8 %copy-done.3 = bf16[128,128]{1,0:T(8,128)(2,1)S(1)} copy-done((bf16[128,128]{1,0:T(8,128)(2,1)S(1)}, bf16[128,128]{1,0:T(8,128)(2,1)}, u32[]{:S(2)}) %copy-start.3) | copy-done | bytes 32792
  25.0 0.0 copy-start.4
  25.0 0.8 %copy-done.4 = bf16[128,128]{1,0:T(8,128)(2,1)S(1)} copy-done((bf16[128,128]{1,0:T(8,128)(2,1)S(1)}, bf16[128,128]{1,0:T(8,128)(2,1)}, u32[]{:S(2)}) %copy-start.4) | copy-done | bytes 32792
  25.7 0.0 copy-start.5
  25.7 0.8 %copy-done.5 = bf16[128,128]{1,0:T(8,128)(2,1)S(1)} copy-done((bf16[128,128]{1,0:T(8,128)(2,1)S(1)}, bf16[128,128]{1,0:T(8,128)(2,1)}, u32[]{:S(2)}) %copy-start.5) | copy-done | bytes 32792
  26.5 0.0 copy-start.6
  26.5 0.8 %copy-done.6 = bf16[128,128]{1,0:T(8,128)(2,1)S(1)} copy-done((bf16[128,128]{1,0:T(8,128)(2,1)S(1)}, bf16[128,128]{1,0:T(8,128)(2,1)}, u32[]{:S(2)}) %copy-start.6) | copy-done | bytes 32792
  27.2 10.7 %shard_map.82 = (f32[2048,128]{1,0:T(8,128)S(1)}, bf16[2048,128]{1,0:T(8,128)(2,1)S(1)}, bf16[2048,128]{1,0:T(8,128)(2,1)S(1)}) custom-call(bf16[2048,128]{1,0:T(8,128)(2,1)S(1)} %bitcast.5, bf16[2048,128]{1,0:T(8,128)(2,1)S(1)} %collective-permute-done.ahead_ref, bf16[2048,128]{1,0:T(8,128)(2,1)S(1)} %collective-permute-done.1.behind_ref, ...), custom_call_target="tpu_custom_call" | custom-call | flops 4294967296 | bytes 8388608 | tf_op jit(solution)/shard_map/pallas_call | solution.py:159
  38.0 5.1 %collective-permute-start.2 = (bf16[2048,128]{1,0:T(8,128)(2,1)S(1)}, bf16[2048,128]{1,0:T(8,128)(2,1)S(1)}, u32[]{:S(2)}, u32[]{:S(2)}) collective-permute-start(bf16[2048,128]{1,0:T(8,128)(2,1)S(1)} %get-tuple-element.9), channel_id=1, source_target_pairs={{0,63},{1,0},{2,1},{3,2},{4,3},{5,4},{6,5},{7,6},{8,7},{9,8},{10,9... | collective-permute-start | bytes 1572872 | tf_op jit(solution)/shard_map/ppermute | solution.py:176
  43.1 0.0 collective-permute-start.3
  43.1 10.3 %collective-permute-done.2 = bf16[2048,128]{1,0:T(8,128)(2,1)S(1)} collective-permute-done((bf16[2048,128]{1,0:T(8,128)(2,1)S(1)}, bf16[2048,128]{1,0:T(8,128)(2,1)S(1)}, u32[]{:S(2)}, u32[]{:S(2)}) %collective-permute-start.2) | collective-permute-done | bytes 524320 | tf_op jit(solution)/shard_map/ppermute | solution.py:176
  53.4 5.5 %collective-permute-done.3 = bf16[2048,128]{1,0:T(8,128)(2,1)S(1)} collective-permute-done((bf16[2048,128]{1,0:T(8,128)(2,1)S(1)}, bf16[2048,128]{1,0:T(8,128)(2,1)S(1)}, u32[]{:S(2)}, u32[]{:S(2)}) %collective-permute-start.3) | collective-permute-done | bytes 524320 | tf_op jit(solution)/shard_map/ppermute | solution.py:176
  59.0 1.1 %add_bitcast_fusion = f32[1,2048,128]{2,1,0:T(8,128)} fusion(bf16[2048,128]{1,0:T(8,128)(2,1)S(1)} %collective-permute-done.3, f32[2048,128]{1,0:T(8,128)S(1)} %get-tuple-element.8, bf16[2048,128]{1,0:T(8,128)(2,1)S(1)} %collective-permute-done.2), kind=kLoop, calls=%fused_computation | loop fusion | flops 1048576 | bytes 3145728 | tf_op jit(solution)/shard_map/broadcast_in_dim | solution.py:186
Async XLA Ops:
  0.0 21.1 %collective-permute-start.1 = (bf16[2048,128]{1,0:T(8,128)(2,1)}, bf16[2048,128]{1,0:T(8,128)(2,1)S(1)}, u32[]{:S(2)}, u32[]{:S(2)}) collective-permute-start(bf16[2048,128]{1,0:T(8,128)(2,1)} %bitcast.3), channel_id=1, source_target_pairs={{0,1},{1,2},{2,3},{3,4},{4,5},{5,6},{6,7},{7,8},{8,9},{9,10},{10,1... | collective-permute-start | bytes 1572872 | tf_op jit(solution)/shard_map/ppermute | solution.py:176
  1.2 19.9 %collective-permute-start = (bf16[2048,128]{1,0:T(8,128)(2,1)}, bf16[2048,128]{1,0:T(8,128)(2,1)S(1)}, u32[]{:S(2)}, u32[]{:S(2)}) collective-permute-start(bf16[2048,128]{1,0:T(8,128)(2,1)} %bitcast.4), channel_id=1, source_target_pairs={{0,62},{1,63},{2,0},{3,1},{4,2},{5,3},{6,4},{7,5},{8,6},{9,7},{10,... | collective-permute-start | bytes 1572872 | tf_op jit(solution)/shard_map/ppermute | solution.py:176
  21.1 1.0 %copy-start = (bf16[1,2048,128]{2,1,0:T(8,128)(2,1)S(1)}, bf16[1,2048,128]{2,1,0:T(8,128)(2,1)}, u32[]{:S(2)}) copy-start(bf16[1,2048,128]{2,1,0:T(8,128)(2,1)} %param.8) | copy-start | bytes 1572868
  22.1 1.0 %copy-start.1 = (bf16[512,512]{1,0:T(8,128)(2,1)S(1)}, bf16[512,512]{1,0:T(8,128)(2,1)}, u32[]{:S(2)}) copy-start(bf16[512,512]{1,0:T(8,128)(2,1)} %constant.20.clone.refs_6_) | copy-start | bytes 1572868
  23.2 1.0 %copy-start.2 = (bf16[512,512]{1,0:T(8,128)(2,1)S(1)}, bf16[512,512]{1,0:T(8,128)(2,1)}, u32[]{:S(2)}) copy-start(bf16[512,512]{1,0:T(8,128)(2,1)} %constant.14.clone.refs_0_) | copy-start | bytes 1572868
  24.2 0.8 %copy-start.3 = (bf16[128,128]{1,0:T(8,128)(2,1)S(1)}, bf16[128,128]{1,0:T(8,128)(2,1)}, u32[]{:S(2)}) copy-start(bf16[128,128]{1,0:T(8,128)(2,1)} %constant.19.clone.refs_5_) | copy-start | bytes 98308
  25.0 0.8 %copy-start.4 = (bf16[128,128]{1,0:T(8,128)(2,1)S(1)}, bf16[128,128]{1,0:T(8,128)(2,1)}, u32[]{:S(2)}) copy-start(bf16[128,128]{1,0:T(8,128)(2,1)} %constant.18.clone.refs_4_) | copy-start | bytes 98308
  25.7 0.8 %copy-start.5 = (bf16[128,128]{1,0:T(8,128)(2,1)S(1)}, bf16[128,128]{1,0:T(8,128)(2,1)}, u32[]{:S(2)}) copy-start(bf16[128,128]{1,0:T(8,128)(2,1)} %constant.16.clone.refs_2_) | copy-start | bytes 98308
  26.5 0.8 %copy-start.6 = (bf16[128,128]{1,0:T(8,128)(2,1)S(1)}, bf16[128,128]{1,0:T(8,128)(2,1)}, u32[]{:S(2)}) copy-start(bf16[128,128]{1,0:T(8,128)(2,1)} %constant.15.clone.refs_1_) | copy-start | bytes 98308
  38.0 15.5 %collective-permute-start.2 = (bf16[2048,128]{1,0:T(8,128)(2,1)S(1)}, bf16[2048,128]{1,0:T(8,128)(2,1)S(1)}, u32[]{:S(2)}, u32[]{:S(2)}) collective-permute-start(bf16[2048,128]{1,0:T(8,128)(2,1)S(1)} %get-tuple-element.9), channel_id=1, source_target_pairs={{0,63},{1,0},{2,1},{3,2},{4,3},{5,4},{6,5},{7,6},{8,7},{9,8},{10,9... | collective-permute-start | bytes 1572872 | tf_op jit(solution)/shard_map/ppermute | solution.py:176
  43.1 15.8 %collective-permute-start.3 = (bf16[2048,128]{1,0:T(8,128)(2,1)S(1)}, bf16[2048,128]{1,0:T(8,128)(2,1)S(1)}, u32[]{:S(2)}, u32[]{:S(2)}) collective-permute-start(bf16[2048,128]{1,0:T(8,128)(2,1)S(1)} %get-tuple-element.10), channel_id=1, source_target_pairs={{0,2},{1,3},{2,4},{3,5},{4,6},{5,7},{6,8},{7,9},{8,10},{9,11},{10,... | collective-permute-start | bytes 1572872 | tf_op jit(solution)/shard_map/ppermute | solution.py:176
where the time goes:
time: 60.6 us; the launch traced here: 60.1 us
  waiting for transfers between devices  27.4 us (45%)
  starting transfers between devices  14.7 us (24%)
  Pallas kernels  10.7 us (18%)
  local copies, waits for them, and re-layouts  6.15 us (10%)
  other arithmetic  1.11 us (2%)
    ppermute x4, waiting for transfers between devices, shifted(): lax.ppermute(x, 'band', [(i, (i + by) % count) for i in range(count)])  27.4 us
    ppermute x4, starting transfers between devices, shifted(): lax.ppermute(x, 'band', [(i, (i + by) % count) for i in range(count)])  14.7 us
    pallas_call x1, Pallas kernels, exchange(): pl.pallas_call(functools.partial(exchange_kernel, steps), out_shape=[jax....  10.7 us
    unnamed x14, local copies, waits for them, and re-layouts  6.15 us
  transfers between devices with their start and end apart: 4, of which 3 were waited for; matrix products, arithmetic and copies ran while one was open for 0% of the time, Pallas kernels for 0%

commit v1 on v0

--- a/solution.py
+++ b/solution.py
@@ -14,6 +14,7 @@
 HALF = 32
 LANES = 128
 SLOTS = 4
+PITCH = 129
 MIXING = 0.25
 
 
@@ -63,7 +64,7 @@
         kernel.reshape(NG * NG, LANES).astype(np.float32),
         as_bf(inverse),
         as_bf(inverse[y_in]),
-        as_bf(back),
+        as_bf(back * np.float32(-MIXING / NG**3)),
     )
 
 
@@ -71,16 +72,53 @@
     return jnp.dot(left, right, preferred_element_type=jnp.float32)
 
 
-def exchange_kernel(steps, own_ref, ahead_ref, behind_ref, *refs):
-    into, y_fwd, x_fwd, kernel, x_inv, y_inv, back, out_ref, to_ahead, to_behind, planes, flat, spec = refs
+def exchange_kernel(steps, *refs):
+    hbm_in, refs = refs[:10], refs[10:]
+    hbm_out, refs = refs[:3], refs[3:]
+    held_in, refs = refs[:10], refs[10:]
+    held_out, refs = refs[:3], refs[3:]
+    planes, spec, flat, in_sem, table_sem, out_sem = refs
+    own_ref, ahead_ref, behind_ref, into, y_fwd, x_fwd, kernel, x_inv, y_inv, back = held_in
+    out_ref, to_ahead, to_behind = held_out
     block, x_unroll = steps
     rows = block * HALF
+    blocks = NG // block
+
+    def part(at):
+        return pl.ds(pl.multiple_of(at * rows, rows), rows)
+
+    def arriving(which, at):
+        return pltpu.make_async_copy(
+            hbm_in[which].at[part(at)], held_in[which].at[part(at)], in_sem.at[which, at]
+        )
+
+    def table(which):
+        return pltpu.make_async_copy(hbm_in[which], held_in[which], table_sem.at[which])
+
+    def leaving(which, at):
+        return pltpu.make_async_copy(
+            held_out[which].at[part(at)], hbm_out[which].at[part(at)], out_sem.at[which, at]
+        )
+
+    table(3).start()
+    for which in range(3):
+        arriving(which, 0).start()
+    table(4).start()
+    for at in range(1, blocks):
+        for which in range(3):
+            arriving(which, at).start()
+    for which in range(5, 10):
+        table(which).start()
+    table(3).wait()
+    table(4).wait()
 
     def wide(ref, base):
         return ref[pl.ds(base, rows), :].astype(jnp.float32)
 
-    @pl.loop(0, NG // block)
+    @pl.loop(0, blocks)
     def _(at):
+        for which in range(3):
+            arriving(which, at).wait()
         base = pl.multiple_of(at * rows, rows)
         own, ahead, behind = (wide(ref, base) for ref in (own_ref, ahead_ref, behind_ref))
         density = [own * own, own * ahead, behind * own, behind * ahead]
@@ -96,8 +134,11 @@
                 )
             second = dot(y_fwd[...], jnp.concatenate(section, axis=1))
             for n in range(2):
-                place = pl.multiple_of((at * block + 2 * pair + n) * LANES, LANES)
+                place = (at * block + 2 * pair + n) * PITCH
                 planes[pl.ds(place, LANES), :] = second[:, n * LANES : (n + 1) * LANES]
+
+    for which in range(5, 10):
+        table(which).wait()
 
     @pl.loop(0, NG // (2 * x_unroll))
     def _(at):
@@ -106,7 +147,7 @@
             section = jnp.concatenate(
                 [
                     jnp.concatenate(
-                        [planes[pl.ds(ky + n + c * NG, NG, stride=LANES), :] for c in range(2)], axis=0
+                        [planes[pl.ds(ky + n + c * NG, NG, stride=PITCH), :] for c in range(2)], axis=0
                     ).astype(jnp.bfloat16)
                     for n in range(2)
                 ],
@@ -120,17 +161,16 @@
             spectrum = (spectrum * weight).astype(jnp.bfloat16)
             back_one = dot(x_inv[...], spectrum)
             for n in range(2):
-                place = pl.multiple_of((ky + n) * LANES, LANES)
-                spec[pl.ds(place, LANES), :] = back_one[:, n * LANES : (n + 1) * LANES]
-
-    @pl.loop(0, NG // block)
+                spec[pl.ds((ky + n) * PITCH, LANES), :] = back_one[:, n * LANES : (n + 1) * LANES]
+
+    @pl.loop(0, blocks)
     def _(at):
         for pair in range(block // 2):
             x = at * block + 2 * pair
             section = jnp.concatenate(
                 [
                     jnp.concatenate(
-                        [spec[pl.ds(x + n + c * NG, NG, stride=LANES), :] for c in range(2)], axis=0
+                        [spec[pl.ds(x + n + c * NG, NG, stride=PITCH), :] for c in range(2)], axis=0
                     ).astype(jnp.bfloat16)
                     for n in range(2)
                 ],
@@ -144,29 +184,40 @@
                         t * HALF : (t + 1) * HALF, n * LANES : (n + 1) * LANES
                     ]
         base = pl.multiple_of(at * rows, rows)
-        field = dot(flat[...], back[...]) * (-MIXING / NG**3)
+        field = dot(flat[...], back[...])
         alone, onward, rearward, across = (field[:, p * LANES : (p + 1) * LANES] for p in range(SLOTS))
         own, ahead, behind = (wide(ref, base) for ref in (own_ref, ahead_ref, behind_ref))
-        out_ref[pl.ds(base, rows), :] = own * alone + ahead * onward + behind * rearward
         to_ahead[pl.ds(base, rows), :] = (own * onward + behind * across).astype(jnp.bfloat16)
         to_behind[pl.ds(base, rows), :] = (own * rearward + ahead * across).astype(jnp.bfloat16)
-
-
-def exchange(own, ahead, behind, steps=(32, 16)):
+        out_ref[pl.ds(base, rows), :] = own * alone + ahead * onward + behind * rearward
+        for which in range(3):
+            leaving(which, at).start()
+
+    for at in range(blocks):
+        for which in range(3):
+            leaving(which, at).wait()
+
+
+def exchange(own, ahead, behind, steps=(32, 32)):
     tables = [jnp.asarray(t) for t in make_tables()]
     operands = [own, ahead, behind, *tables]
-    block = pl.BlockSpec(memory_space=pltpu.VMEM)
+    outputs = [jax.ShapeDtypeStruct(own.shape, t) for t in (jnp.float32, jnp.bfloat16, jnp.bfloat16)]
+    blocks = NG // steps[0]
     return pl.pallas_call(
         functools.partial(exchange_kernel, steps),
-        out_shape=[jax.ShapeDtypeStruct(own.shape, t) for t in (jnp.float32, jnp.bfloat16, jnp.bfloat16)],
-        in_specs=[block] * len(operands),
-        out_specs=[block] * 3,
-        scratch_shapes=[
-            pltpu.VMEM((NG * LANES, LANES), jnp.float32),
+        out_shape=outputs,
+        in_specs=[pl.BlockSpec(memory_space=pl.ANY)] * len(operands),
+        out_specs=[pl.BlockSpec(memory_space=pl.ANY)] * 3,
+        scratch_shapes=[pltpu.VMEM(x.shape, x.dtype) for x in operands + outputs]
+        + [
+            pltpu.VMEM((NG * PITCH, LANES), jnp.float32),
+            pltpu.VMEM((NG * PITCH, LANES), jnp.float32),
             pltpu.VMEM((steps[0] * HALF, SLOTS * LANES), jnp.bfloat16),
-            pltpu.VMEM((NG * LANES, LANES), jnp.float32),
+            pltpu.SemaphoreType.DMA((3, blocks)),
+            pltpu.SemaphoreType.DMA((10,)),
+            pltpu.SemaphoreType.DMA((3, blocks)),
         ],
-        compiler_params=pltpu.CompilerParams(vmem_limit_bytes=48 * 1024 * 1024),
+        compiler_params=pltpu.CompilerParams(vmem_limit_bytes=60 * 1024 * 1024),
         cost_estimate=pl.CostEstimate(flops=2**32, bytes_accessed=8 << 20, transcendentals=0),
     )(*operands)
 

time: 60.6 us -> 53.3 us (0.88)
  local copies, waits for them, and re-layouts: 6.15 us -> 1.58 us
  Pallas kernels: 10.7 us -> 7.78 us
  other arithmetic: 1.11 us -> 2.33 us
  starting transfers between devices: 14.7 us -> 13.9 us
    unnamed x14 -> x4, local copies, waits for them, and re-layouts: 6.15 us -> 1.58 us
    pallas_call x1, Pallas kernels: 10.7 us -> 7.78 us  [exchange(): pl.pallas_call(functools.partial(exchange_kernel, steps), out_shape=outpu...]
    broadcast_in_dim x1, other arithmetic: 1.11 us -> 2.33 us  [local(): return total[None]]
    ppermute x4, starting transfers between devices: 14.7 us -> 13.9 us  [shifted(): lax.ppermute(x, 'band', [(i, (i + by) % count) for i in range(count)])]
where the time goes in v1:
time: 53.3 us; the launch traced here: 53.2 us
  waiting for transfers between devices  27.6 us (52%)
  starting transfers between devices  13.9 us (26%)
  Pallas kernels  7.78 us (15%)
  other arithmetic  2.33 us (4%)
  local copies, waits for them, and re-layouts  1.58 us (3%)
    ppermute x4, waiting for transfers between devices, shifted(): lax.ppermute(x, 'band', [(i, (i + by) % count) for i in range(count)])  27.6 us
    ppermute x4, starting transfers between devices, shifted(): lax.ppermute(x, 'band', [(i, (i + by) % count) for i in range(count)])  13.9 us
    pallas_call x1, Pallas kernels, exchange(): pl.pallas_call(functools.partial(exchange_kernel, steps), out_shape=outpu...  7.78 us
    broadcast_in_dim x1, other arithmetic, local(): return total[None]  2.33 us
    unnamed x4, local copies, waits for them, and re-layouts  1.58 us
  transfers between devices with their start and end apart: 4, of which 3 were waited for; matrix products, arithmetic and copies ran while one was open for 0% of the time, Pallas kernels for 0%

profile of v1, /device:TPU:4, one launch (start us, length us, event | category | flops | bytes accessed | tf_op | source)
XLA Modules:
  0.0 53.2 jit_solution(13737976641338363692)
XLA Ops:
  0.0 1.2 %collective-permute-start.1 = (bf16[2048,128]{1,0:T(8,128)(2,1)}, bf16[2048,128]{1,0:T(8,128)(2,1)S(1)}, u32[]{:S(2)}, u32[]{:S(2)}) collective-permute-start(bf16[2048,128]{1,0:T(8,128)(2,1)} %bitcast.3), channel_id=1, source_target_pairs={{0,1},{1,2},{2,3},{3,4},{4,5},{5,6},{6,7},{7,8},{8,9},{9,10},{10,1... | collective-permute-start | bytes 1572872 | tf_op jit(solution)/shard_map/ppermute | solution.py:227
  1.2 8.3 %collective-permute-start = (bf16[2048,128]{1,0:T(8,128)(2,1)}, bf16[2048,128]{1,0:T(8,128)(2,1)S(1)}, u32[]{:S(2)}, u32[]{:S(2)}) collective-permute-start(bf16[2048,128]{1,0:T(8,128)(2,1)} %bitcast.4), channel_id=1, source_target_pairs={{0,62},{1,63},{2,0},{3,1},{4,2},{5,3},{6,4},{7,5},{8,6},{9,7},{10,... | collective-permute-start | bytes 1572872 | tf_op jit(solution)/shard_map/ppermute | solution.py:227
  9.5 11.6 %collective-permute-done.1.refs_2_ = bf16[2048,128]{1,0:T(8,128)(2,1)S(1)} collective-permute-done((bf16[2048,128]{1,0:T(8,128)(2,1)}, bf16[2048,128]{1,0:T(8,128)(2,1)S(1)}, u32[]{:S(2)}, u32[]{:S(2)}) %collective-permute-start.1) | collective-permute-done | bytes 524320 | tf_op jit(solution)/shard_map/ppermute | solution.py:227
  21.1 0.0 copy-start
  21.1 0.0 collective-permute-done.refs_1_
  21.1 0.8 %copy-done = bf16[2048,128]{1,0:T(8,128)(2,1)} copy-done((bf16[2048,128]{1,0:T(8,128)(2,1)}, bf16[2048,128]{1,0:T(8,128)(2,1)S(1)}, u32[]{:S(2)}) %copy-start) | copy-done | bytes 524312
  21.9 0.0 copy-start.1
  21.9 0.8 %copy-done.1 = bf16[2048,128]{1,0:T(8,128)(2,1)} copy-done((bf16[2048,128]{1,0:T(8,128)(2,1)}, bf16[2048,128]{1,0:T(8,128)(2,1)S(1)}, u32[]{:S(2)}) %copy-start.1) | copy-done | bytes 524312
  22.7 7.8 %shard_map.82 = (f32[2048,128]{1,0:T(8,128)}, bf16[2048,128]{1,0:T(8,128)(2,1)}, bf16[2048,128]{1,0:T(8,128)(2,1)}) custom-call(bf16[2048,128]{1,0:T(8,128)(2,1)} %bitcast.5, bf16[2048,128]{1,0:T(8,128)(2,1)} %copy-done.1, bf16[2048,128]{1,0:T(8,128)(2,1)} %copy-done, bf16[512,512]{1,0:T(8,128)(2,1)} %constant.14.clone.refs_3_, ...), custom_call_target="tpu_custom_call" | custom-call | flops 4294967296 | bytes 8388608 | tf_op jit(solution)/shard_map/pallas_call | solution.py:206
  30.5 4.3 %collective-permute-start.2 = (bf16[2048,128]{1,0:T(8,128)(2,1)}, bf16[2048,128]{1,0:T(8,128)(2,1)S(1)}, u32[]{:S(2)}, u32[]{:S(2)}) collective-permute-start(bf16[2048,128]{1,0:T(8,128)(2,1)} %get-tuple-element.9), channel_id=1, source_target_pairs={{0,63},{1,0},{2,1},{3,2},{4,3},{5,4},{6,5},{7,6},{8,7},{9,8},{10,9... | collective-permute-start | bytes 1572872 | tf_op jit(solution)/shard_map/ppermute | solution.py:227
  34.8 0.0 collective-permute-start.3
  34.8 10.6 %collective-permute-done.2 = bf16[2048,128]{1,0:T(8,128)(2,1)S(1)} collective-permute-done((bf16[2048,128]{1,0:T(8,128)(2,1)}, bf16[2048,128]{1,0:T(8,128)(2,1)S(1)}, u32[]{:S(2)}, u32[]{:S(2)}) %collective-permute-start.2) | collective-permute-done | bytes 524320 | tf_op jit(solution)/shard_map/ppermute | solution.py:227
  45.4 5.4 %collective-permute-done.3 = bf16[2048,128]{1,0:T(8,128)(2,1)S(1)} collective-permute-done((bf16[2048,128]{1,0:T(8,128)(2,1)}, bf16[2048,128]{1,0:T(8,128)(2,1)S(1)}, u32[]{:S(2)}, u32[]{:S(2)}) %collective-permute-start.3) | collective-permute-done | bytes 524320 | tf_op jit(solution)/shard_map/ppermute | solution.py:227
  50.8 2.3 %add_bitcast_fusion = f32[1,2048,128]{2,1,0:T(8,128)} fusion(bf16[2048,128]{1,0:T(8,128)(2,1)S(1)} %collective-permute-done.3, f32[2048,128]{1,0:T(8,128)} %get-tuple-element.8, bf16[2048,128]{1,0:T(8,128)(2,1)S(1)} %collective-permute-done.2), kind=kLoop, calls=%fused_computation | loop fusion | flops 1048576 | bytes 3145728 | tf_op jit(solution)/shard_map/broadcast_in_dim | solution.py:237
Async XLA Ops:
  0.0 21.1 %collective-permute-start.1 = (bf16[2048,128]{1,0:T(8,128)(2,1)}, bf16[2048,128]{1,0:T(8,128)(2,1)S(1)}, u32[]{:S(2)}, u32[]{:S(2)}) collective-permute-start(bf16[2048,128]{1,0:T(8,128)(2,1)} %bitcast.3), channel_id=1, source_target_pairs={{0,1},{1,2},{2,3},{3,4},{4,5},{5,6},{6,7},{7,8},{8,9},{9,10},{10,1... | collective-permute-start | bytes 1572872 | tf_op jit(solution)/shard_map/ppermute | solution.py:227
  1.2 19.9 %collective-permute-start = (bf16[2048,128]{1,0:T(8,128)(2,1)}, bf16[2048,128]{1,0:T(8,128)(2,1)S(1)}, u32[]{:S(2)}, u32[]{:S(2)}) collective-permute-start(bf16[2048,128]{1,0:T(8,128)(2,1)} %bitcast.4), channel_id=1, source_target_pairs={{0,62},{1,63},{2,0},{3,1},{4,2},{5,3},{6,4},{7,5},{8,6},{9,7},{10,... | collective-permute-start | bytes 1572872 | tf_op jit(solution)/shard_map/ppermute | solution.py:227
  21.1 0.8 %copy-start = (bf16[2048,128]{1,0:T(8,128)(2,1)}, bf16[2048,128]{1,0:T(8,128)(2,1)S(1)}, u32[]{:S(2)}) copy-start(bf16[2048,128]{1,0:T(8,128)(2,1)S(1)} %collective-permute-done.1.refs_2_) | copy-start | bytes 1572868
  21.9 0.8 %copy-start.1 = (bf16[2048,128]{1,0:T(8,128)(2,1)}, bf16[2048,128]{1,0:T(8,128)(2,1)S(1)}, u32[]{:S(2)}) copy-start(bf16[2048,128]{1,0:T(8,128)(2,1)S(1)} %collective-permute-done.refs_1_) | copy-start | bytes 1572868
  30.5 15.0 %collective-permute-start.2 = (bf16[2048,128]{1,0:T(8,128)(2,1)}, bf16[2048,128]{1,0:T(8,128)(2,1)S(1)}, u32[]{:S(2)}, u32[]{:S(2)}) collective-permute-start(bf16[2048,128]{1,0:T(8,128)(2,1)} %get-tuple-element.9), channel_id=1, source_target_pairs={{0,63},{1,0},{2,1},{3,2},{4,3},{5,4},{6,5},{7,6},{8,7},{9,8},{10,9... | collective-permute-start | bytes 1572872 | tf_op jit(solution)/shard_map/ppermute | solution.py:227
  34.8 16.0 %collective-permute-start.3 = (bf16[2048,128]{1,0:T(8,128)(2,1)}, bf16[2048,128]{1,0:T(8,128)(2,1)S(1)}, u32[]{:S(2)}, u32[]{:S(2)}) collective-permute-start(bf16[2048,128]{1,0:T(8,128)(2,1)} %get-tuple-element.10), channel_id=1, source_target_pairs={{0,2},{1,3},{2,4},{3,5},{4,6},{5,7},{6,8},{7,9},{8,10},{9,11},{10,... | collective-permute-start | bytes 1572872 | tf_op jit(solution)/shard_map/ppermute | solution.py:227

commit v2 on v0

--- a/solution.py
+++ b/solution.py
@@ -14,6 +14,7 @@
 HALF = 32
 LANES = 128
 SLOTS = 4
+PITCH = 129
 MIXING = 0.25
 
 
@@ -63,7 +64,7 @@
         kernel.reshape(NG * NG, LANES).astype(np.float32),
         as_bf(inverse),
         as_bf(inverse[y_in]),
-        as_bf(back),
+        as_bf(back * np.float32(-MIXING / NG**3)),
     )
 
 
@@ -72,14 +73,15 @@
 
 
 def exchange_kernel(steps, own_ref, ahead_ref, behind_ref, *refs):
-    into, y_fwd, x_fwd, kernel, x_inv, y_inv, back, out_ref, to_ahead, to_behind, planes, flat, spec = refs
+    into, y_fwd, x_fwd, kernel, x_inv, y_inv, back, out_ref, to_ahead, to_behind, planes, spec, flat = refs
     block, x_unroll = steps
     rows = block * HALF
+    blocks = NG // block
 
     def wide(ref, base):
         return ref[pl.ds(base, rows), :].astype(jnp.float32)
 
-    @pl.loop(0, NG // block)
+    @pl.loop(0, blocks)
     def _(at):
         base = pl.multiple_of(at * rows, rows)
         own, ahead, behind = (wide(ref, base) for ref in (own_ref, ahead_ref, behind_ref))
@@ -96,7 +98,7 @@
                 )
             second = dot(y_fwd[...], jnp.concatenate(section, axis=1))
             for n in range(2):
-                place = pl.multiple_of((at * block + 2 * pair + n) * LANES, LANES)
+                place = (at * block + 2 * pair + n) * PITCH
                 planes[pl.ds(place, LANES), :] = second[:, n * LANES : (n + 1) * LANES]
 
     @pl.loop(0, NG // (2 * x_unroll))
@@ -106,7 +108,7 @@
             section = jnp.concatenate(
                 [
                     jnp.concatenate(
-                        [planes[pl.ds(ky + n + c * NG, NG, stride=LANES), :] for c in range(2)], axis=0
+                        [planes[pl.ds(ky + n + c * NG, NG, stride=PITCH), :] for c in range(2)], axis=0
                     ).astype(jnp.bfloat16)
                     for n in range(2)
                 ],
@@ -120,17 +122,16 @@
             spectrum = (spectrum * weight).astype(jnp.bfloat16)
             back_one = dot(x_inv[...], spectrum)
             for n in range(2):
-                place = pl.multiple_of((ky + n) * LANES, LANES)
-                spec[pl.ds(place, LANES), :] = back_one[:, n * LANES : (n + 1) * LANES]
-
-    @pl.loop(0, NG // block)
+                spec[pl.ds((ky + n) * PITCH, LANES), :] = back_one[:, n * LANES : (n + 1) * LANES]
+
+    @pl.loop(0, blocks)
     def _(at):
         for pair in range(block // 2):
             x = at * block + 2 * pair
             section = jnp.concatenate(
                 [
                     jnp.concatenate(
-                        [spec[pl.ds(x + n + c * NG, NG, stride=LANES), :] for c in range(2)], axis=0
+                        [spec[pl.ds(x + n + c * NG, NG, stride=PITCH), :] for c in range(2)], axis=0
                     ).astype(jnp.bfloat16)
                     for n in range(2)
                 ],
@@ -144,29 +145,51 @@
                         t * HALF : (t + 1) * HALF, n * LANES : (n + 1) * LANES
                     ]
         base = pl.multiple_of(at * rows, rows)
-        field = dot(flat[...], back[...]) * (-MIXING / NG**3)
+        field = dot(flat[...], back[...])
         alone, onward, rearward, across = (field[:, p * LANES : (p + 1) * LANES] for p in range(SLOTS))
         own, ahead, behind = (wide(ref, base) for ref in (own_ref, ahead_ref, behind_ref))
-        out_ref[pl.ds(base, rows), :] = own * alone + ahead * onward + behind * rearward
         to_ahead[pl.ds(base, rows), :] = (own * onward + behind * across).astype(jnp.bfloat16)
         to_behind[pl.ds(base, rows), :] = (own * rearward + ahead * across).astype(jnp.bfloat16)
-
-
-def exchange(own, ahead, behind, steps=(32, 16)):
+        out_ref[pl.ds(base, rows), :] = own * alone + ahead * onward + behind * rearward
+
+
+def hold_kernel(*refs):
+    count = len(refs) // 2
+    sources, held, sem = refs[:count], refs[count : 2 * count], refs[2 * count]
+    copies = [pltpu.make_async_copy(s, h, sem.at[n]) for n, (s, h) in enumerate(zip(sources, held))]
+    for copy in copies:
+        copy.start()
+    for copy in copies:
+        copy.wait()
+
+
+def held_in_vmem(arrays):
+    return pl.pallas_call(
+        hold_kernel,
+        out_shape=[pltpu.VMEM(x.shape, x.dtype) for x in arrays],
+        in_specs=[pl.BlockSpec(memory_space=pl.ANY)] * len(arrays),
+        out_specs=[pl.BlockSpec(memory_space=pltpu.VMEM)] * len(arrays),
+        scratch_shapes=[pltpu.SemaphoreType.DMA((len(arrays),))],
+        compiler_params=pltpu.CompilerParams(vmem_limit_bytes=1024 * 1024),
+        cost_estimate=pl.CostEstimate(flops=0, bytes_accessed=8 << 20, transcendentals=0),
+    )(*arrays)
+
+
+def exchange(own, ahead, behind, steps=(32, 32)):
     tables = [jnp.asarray(t) for t in make_tables()]
+    own, *tables = held_in_vmem([own, *tables])
     operands = [own, ahead, behind, *tables]
-    block = pl.BlockSpec(memory_space=pltpu.VMEM)
     return pl.pallas_call(
         functools.partial(exchange_kernel, steps),
         out_shape=[jax.ShapeDtypeStruct(own.shape, t) for t in (jnp.float32, jnp.bfloat16, jnp.bfloat16)],
-        in_specs=[block] * len(operands),
-        out_specs=[block] * 3,
+        in_specs=[pl.BlockSpec(memory_space=pltpu.VMEM)] * len(operands),
+        out_specs=[pl.BlockSpec(memory_space=pltpu.VMEM)] * 3,
         scratch_shapes=[
-            pltpu.VMEM((NG * LANES, LANES), jnp.float32),
+            pltpu.VMEM((NG * PITCH, LANES), jnp.float32),
+            pltpu.VMEM((NG * PITCH, LANES), jnp.float32),
             pltpu.VMEM((steps[0] * HALF, SLOTS * LANES), jnp.bfloat16),
-            pltpu.VMEM((NG * LANES, LANES), jnp.float32),
         ],
-        compiler_params=pltpu.CompilerParams(vmem_limit_bytes=48 * 1024 * 1024),
+        compiler_params=pltpu.CompilerParams(vmem_limit_bytes=24 * 1024 * 1024),
         cost_estimate=pl.CostEstimate(flops=2**32, bytes_accessed=8 << 20, transcendentals=0),
     )(*operands)
 

time: 60.6 us -> 49 us (0.81)
  waiting for transfers between devices: 27.4 us -> 19.1 us
  Pallas kernels: 10.7 us -> 5.82 us
  local copies, waits for them, and re-layouts: 6.15 us -> 7.74 us
    ppermute x4, waiting for transfers between devices: 27.4 us -> 19.1 us  [shifted(): lax.ppermute(x, 'band', [(i, (i + by) % count) for i in range(count)])]
    pallas_call x1, Pallas kernels: 10.7 us -> 5.33 us  [exchange(): pl.pallas_call(functools.partial(exchange_kernel, steps), out_shape=[jax....]
    unnamed x14 -> x16, local copies, waits for them, and re-layouts: 6.15 us -> 7.74 us
  transfers between devices with their start and end apart: 4 -> 4, of which waited for: 3 -> 3; matrix products, arithmetic and copies ran while one was open for 0% -> 0% of each run, Pallas kernels for 0% -> 1%
where the time goes in v2:
time: 49 us; the launch traced here: 48.5 us
  waiting for transfers between devices  19.1 us (39%)
  starting transfers between devices  14.6 us (30%)
  local copies, waits for them, and re-layouts  7.74 us (16%)
  Pallas kernels  5.82 us (12%)
  other arithmetic  1.11 us (2%)
    ppermute x4, waiting for transfers between devices, shifted(): lax.ppermute(x, 'band', [(i, (i + by) % count) for i in range(count)])  19.1 us
    ppermute x4, starting transfers between devices, shifted(): lax.ppermute(x, 'band', [(i, (i + by) % count) for i in range(count)])  14.6 us
    unnamed x16, local copies, waits for them, and re-layouts  7.74 us
    pallas_call x1, Pallas kernels, exchange(): pl.pallas_call(functools.partial(exchange_kernel, steps), out_shape=[jax....  5.33 us
    broadcast_in_dim x1, other arithmetic, local(): return total[None]  1.11 us
  transfers between devices with their start and end apart: 4, of which 3 were waited for; matrix products, arithmetic and copies ran while one was open for 0% of the time, Pallas kernels for 1%

profile of v2, /device:TPU:4, one launch (start us, length us, event | category | flops | bytes accessed | tf_op | source)
XLA Modules:
  0.0 48.5 jit_solution(7847688053391675839)
XLA Ops:
  0.0 1.2 %collective-permute-start.1 = (bf16[2048,128]{1,0:T(8,128)(2,1)}, bf16[2048,128]{1,0:T(8,128)(2,1)S(1)}, u32[]{:S(2)}, u32[]{:S(2)}) collective-permute-start(bf16[2048,128]{1,0:T(8,128)(2,1)} %bitcast.3), channel_id=1, source_target_pairs={{0,1},{1,2},{2,3},{3,4},{4,5},{5,6},{6,7},{7,8},{8,9},{9,10},{10,1... | collective-permute-start | bytes 1572872 | tf_op jit(solution)/shard_map/ppermute | solution.py:199
  1.2 8.3 %collective-permute-start = (bf16[2048,128]{1,0:T(8,128)(2,1)}, bf16[2048,128]{1,0:T(8,128)(2,1)S(1)}, u32[]{:S(2)}, u32[]{:S(2)}) collective-permute-start(bf16[2048,128]{1,0:T(8,128)(2,1)} %bitcast.4), channel_id=1, source_target_pairs={{0,62},{1,63},{2,0},{3,1},{4,2},{5,3},{6,4},{7,5},{8,6},{9,7},{10,... | collective-permute-start | bytes 1572872 | tf_op jit(solution)/shard_map/ppermute | solution.py:199
  9.5 0.0 copy-start
  9.5 1.6 %copy-done = f32[4096,128]{1,0:T(8,128)S(1)} copy-done((f32[4096,128]{1,0:T(8,128)S(1)}, f32[4096,128]{1,0:T(8,128)}, u32[]{:S(2)}) %copy-start) | copy-done | bytes 2097176
  11.1 0.0 copy-start.1
  11.1 1.0 %copy-done.1 = bf16[1,2048,128]{2,1,0:T(8,128)(2,1)S(1)} copy-done((bf16[1,2048,128]{2,1,0:T(8,128)(2,1)S(1)}, bf16[1,2048,128]{2,1,0:T(8,128)(2,1)}, u32[]{:S(2)}) %copy-start.1) | copy-done | bytes 524312
  12.1 0.0 copy-start.2
  12.1 1.0 %copy-done.2 = bf16[512,512]{1,0:T(8,128)(2,1)S(1)} copy-done((bf16[512,512]{1,0:T(8,128)(2,1)S(1)}, bf16[512,512]{1,0:T(8,128)(2,1)}, u32[]{:S(2)}) %copy-start.2) | copy-done | bytes 524312
  13.2 0.0 copy-start.3
  13.2 1.0 %copy-done.3 = bf16[512,512]{1,0:T(8,128)(2,1)S(1)} copy-done((bf16[512,512]{1,0:T(8,128)(2,1)S(1)}, bf16[512,512]{1,0:T(8,128)(2,1)}, u32[]{:S(2)}) %copy-start.3) | copy-done | bytes 524312
  14.2 0.0 copy-start.4
  14.2 0.8 %copy-done.4 = bf16[128,128]{1,0:T(8,128)(2,1)S(1)} copy-done((bf16[128,128]{1,0:T(8,128)(2,1)S(1)}, bf16[128,128]{1,0:T(8,128)(2,1)}, u32[]{:S(2)}) %copy-start.4) | copy-done | bytes 32792
  15.0 0.0 copy-start.5
  15.0 0.8 %copy-done.5 = bf16[128,128]{1,0:T(8,128)(2,1)S(1)} copy-done((bf16[128,128]{1,0:T(8,128)(2,1)S(1)}, bf16[128,128]{1,0:T(8,128)(2,1)}, u32[]{:S(2)}) %copy-start.5) | copy-done | bytes 32792
  15.7 0.0 copy-start.6
  15.7 0.8 %copy-done.6 = bf16[128,128]{1,0:T(8,128)(2,1)S(1)} copy-done((bf16[128,128]{1,0:T(8,128)(2,1)S(1)}, bf16[128,128]{1,0:T(8,128)(2,1)}, u32[]{:S(2)}) %copy-start.6) | copy-done | bytes 32792
  16.5 0.0 copy-start.7
  16.5 0.8 %copy-done.7 = bf16[128,128]{1,0:T(8,128)(2,1)S(1)} copy-done((bf16[128,128]{1,0:T(8,128)(2,1)S(1)}, bf16[128,128]{1,0:T(8,128)(2,1)}, u32[]{:S(2)}) %copy-start.7) | copy-done | bytes 32792
  17.3 0.5 %shard_map.82 = (bf16[2048,128]{1,0:T(8,128)(2,1)S(1)}, bf16[512,512]{1,0:T(8,128)(2,1)S(1)}, bf16[128,128]{1,0:T(8,128)(2,1)S(1)}, bf16[128,128]{1,0:T(8,128)(2...) custom-call(bf16[2048,128]{1,0:T(8,128)(2,1)S(1)} %bitcast.5, ...), custom_call_target="tpu_custom_call" | custom-call | bytes 8388608 | tf_op jit(solution)/shard_map/pallas_call | solution.py:167
  17.8 3.3 %collective-permute-done.1.behind_ref = bf16[2048,128]{1,0:T(8,128)(2,1)S(1)} collective-permute-done((bf16[2048,128]{1,0:T(8,128)(2,1)}, bf16[2048,128]{1,0:T(8,128)(2,1)S(1)}, u32[]{:S(2)}, u32[]{:S(2)}) %collective-permute-start.1) | collective-permute-done | bytes 524320 | tf_op jit(solution)/shard_map/ppermute | solution.py:199
  21.1 0.0 collective-permute-done.ahead_ref
  21.1 5.3 %shard_map.83 = (f32[2048,128]{1,0:T(8,128)S(1)}, bf16[2048,128]{1,0:T(8,128)(2,1)S(1)}, bf16[2048,128]{1,0:T(8,128)(2,1)S(1)}) custom-call(bf16[2048,128]{1,0:T(8,128)(2,1)S(1)} %get-tuple-element.16.own_ref, bf16[2048,128]{1,0:T(8,128)(2,1)S(1)} %collective-permute-done.ahead_ref, bf16[2048,128]{1,0:T(8,128)(2,1)S(1)} %collective-permute-done.1.behind_ref, ...), custom_call_target="tpu_custom_call" | custom-call | flops 4294967296 | bytes 8388608 | tf_op jit(solution)/shard_map/pallas_call | solution.py:182
  26.4 5.1 %collective-permute-start.2 = (bf16[2048,128]{1,0:T(8,128)(2,1)S(1)}, bf16[2048,128]{1,0:T(8,128)(2,1)S(1)}, u32[]{:S(2)}, u32[]{:S(2)}) collective-permute-start(bf16[2048,128]{1,0:T(8,128)(2,1)S(1)} %get-tuple-element.25), channel_id=1, source_target_pairs={{0,63},{1,0},{2,1},{3,2},{4,3},{5,4},{6,5},{7,6},{8,7},{9,8},{10,9... | collective-permute-start | bytes 1572872 | tf_op jit(solution)/shard_map/ppermute | solution.py:199
  31.5 0.0 collective-permute-start.3
  31.6 10.3 %collective-permute-done.2 = bf16[2048,128]{1,0:T(8,128)(2,1)S(1)} collective-permute-done((bf16[2048,128]{1,0:T(8,128)(2,1)S(1)}, bf16[2048,128]{1,0:T(8,128)(2,1)S(1)}, u32[]{:S(2)}, u32[]{:S(2)}) %collective-permute-start.2) | collective-permute-done | bytes 524320 | tf_op jit(solution)/shard_map/ppermute | solution.py:199
  41.9 5.5 %collective-permute-done.3 = bf16[2048,128]{1,0:T(8,128)(2,1)S(1)} collective-permute-done((bf16[2048,128]{1,0:T(8,128)(2,1)S(1)}, bf16[2048,128]{1,0:T(8,128)(2,1)S(1)}, u32[]{:S(2)}, u32[]{:S(2)}) %collective-permute-start.3) | collective-permute-done | bytes 524320 | tf_op jit(solution)/shard_map/ppermute | solution.py:199
  47.4 1.1 %add_bitcast_fusion = f32[1,2048,128]{2,1,0:T(8,128)} fusion(bf16[2048,128]{1,0:T(8,128)(2,1)S(1)} %collective-permute-done.3, f32[2048,128]{1,0:T(8,128)S(1)} %get-tuple-element.24, bf16[2048,128]{1,0:T(8,128)(2,1)S(1)} %collective-permute-done.2), kind=kLoop, calls=%fused_computation | loop fusion | flops 1048576 | bytes 3145728 | tf_op jit(solution)/shard_map/broadcast_in_dim | solution.py:209
Async XLA Ops:
  0.0 21.1 %collective-permute-start.1 = (bf16[2048,128]{1,0:T(8,128)(2,1)}, bf16[2048,128]{1,0:T(8,128)(2,1)S(1)}, u32[]{:S(2)}, u32[]{:S(2)}) collective-permute-start(bf16[2048,128]{1,0:T(8,128)(2,1)} %bitcast.3), channel_id=1, source_target_pairs={{0,1},{1,2},{2,3},{3,4},{4,5},{5,6},{6,7},{7,8},{8,9},{9,10},{10,1... | collective-permute-start | bytes 1572872 | tf_op jit(solution)/shard_map/ppermute | solution.py:199
  1.2 19.9 %collective-permute-start = (bf16[2048,128]{1,0:T(8,128)(2,1)}, bf16[2048,128]{1,0:T(8,128)(2,1)S(1)}, u32[]{:S(2)}, u32[]{:S(2)}) collective-permute-start(bf16[2048,128]{1,0:T(8,128)(2,1)} %bitcast.4), channel_id=1, source_target_pairs={{0,62},{1,63},{2,0},{3,1},{4,2},{5,3},{6,4},{7,5},{8,6},{9,7},{10,... | collective-permute-start | bytes 1572872 | tf_op jit(solution)/shard_map/ppermute | solution.py:199
  9.5 1.6 %copy-start = (f32[4096,128]{1,0:T(8,128)S(1)}, f32[4096,128]{1,0:T(8,128)}, u32[]{:S(2)}) copy-start(f32[4096,128]{1,0:T(8,128)} %constant.17.clone.refs_4_) | copy-start | bytes 6291460
  11.1 1.0 %copy-start.1 = (bf16[1,2048,128]{2,1,0:T(8,128)(2,1)S(1)}, bf16[1,2048,128]{2,1,0:T(8,128)(2,1)}, u32[]{:S(2)}) copy-start(bf16[1,2048,128]{2,1,0:T(8,128)(2,1)} %param.8) | copy-start | bytes 1572868
  12.1 1.0 %copy-start.2 = (bf16[512,512]{1,0:T(8,128)(2,1)S(1)}, bf16[512,512]{1,0:T(8,128)(2,1)}, u32[]{:S(2)}) copy-start(bf16[512,512]{1,0:T(8,128)(2,1)} %constant.20.clone.refs_7_) | copy-start | bytes 1572868
  13.2 1.0 %copy-start.3 = (bf16[512,512]{1,0:T(8,128)(2,1)S(1)}, bf16[512,512]{1,0:T(8,128)(2,1)}, u32[]{:S(2)}) copy-start(bf16[512,512]{1,0:T(8,128)(2,1)} %constant.14.clone.refs_1_) | copy-start | bytes 1572868
  14.2 0.8 %copy-start.4 = (bf16[128,128]{1,0:T(8,128)(2,1)S(1)}, bf16[128,128]{1,0:T(8,128)(2,1)}, u32[]{:S(2)}) copy-start(bf16[128,128]{1,0:T(8,128)(2,1)} %constant.19.clone.refs_6_) | copy-start | bytes 98308
  15.0 0.8 %copy-start.5 = (bf16[128,128]{1,0:T(8,128)(2,1)S(1)}, bf16[128,128]{1,0:T(8,128)(2,1)}, u32[]{:S(2)}) copy-start(bf16[128,128]{1,0:T(8,128)(2,1)} %constant.18.clone.refs_5_) | copy-start | bytes 98308
  15.7 0.8 %copy-start.6 = (bf16[128,128]{1,0:T(8,128)(2,1)S(1)}, bf16[128,128]{1,0:T(8,128)(2,1)}, u32[]{:S(2)}) copy-start(bf16[128,128]{1,0:T(8,128)(2,1)} %constant.16.clone.refs_3_) | copy-start | bytes 98308
  16.5 0.8 %copy-start.7 = (bf16[128,128]{1,0:T(8,128)(2,1)S(1)}, bf16[128,128]{1,0:T(8,128)(2,1)}, u32[]{:S(2)}) copy-start(bf16[128,128]{1,0:T(8,128)(2,1)} %constant.15.clone.refs_2_) | copy-start | bytes 98308
  26.4 15.4 %collective-permute-start.2 = (bf16[2048,128]{1,0:T(8,128)(2,1)S(1)}, bf16[2048,128]{1,0:T(8,128)(2,1)S(1)}, u32[]{:S(2)}, u32[]{:S(2)}) collective-permute-start(bf16[2048,128]{1,0:T(8,128)(2,1)S(1)} %get-tuple-element.25), channel_id=1, source_target_pairs={{0,63},{1,0},{2,1},{3,2},{4,3},{5,4},{6,5},{7,6},{8,7},{9,8},{10,9... | collective-permute-start | bytes 1572872 | tf_op jit(solution)/shard_map/ppermute | solution.py:199
  31.5 15.8 %collective-permute-start.3 = (bf16[2048,128]{1,0:T(8,128)(2,1)S(1)}, bf16[2048,128]{1,0:T(8,128)(2,1)S(1)}, u32[]{:S(2)}, u32[]{:S(2)}) collective-permute-start(bf16[2048,128]{1,0:T(8,128)(2,1)S(1)} %get-tuple-element.26), channel_id=1, source_target_pairs={{0,2},{1,3},{2,4},{3,5},{4,6},{5,7},{6,8},{7,9},{8,10},{9,11},{10,... | collective-permute-start | bytes 1572872 | tf_op jit(solution)/shard_map/ppermute | solution.py:199

commit v3 on v2

--- a/solution.py
+++ b/solution.py
@@ -204,8 +204,8 @@
     behind = shifted(own, 1)
     ahead = shifted(own, -2)
     total, to_ahead, to_behind = exchange(own, ahead, behind)
+    total = total + shifted(to_ahead, 2).astype(jnp.float32)
     total = total + shifted(to_behind, -1).astype(jnp.float32)
-    total = total + shifted(to_ahead, 2).astype(jnp.float32)
     return total[None]
 
 

time: 49 us -> 44.6 us (0.910)
  waiting for transfers between devices: 19.1 us -> 14.6 us
    ppermute x4, waiting for transfers between devices: 19.1 us -> 14.6 us  [shifted(): lax.ppermute(x, 'band', [(i, (i + by) % count) for i in range(count)])]
  transfers between devices with their start and end apart: 4 -> 4, of which waited for: 3 -> 2; matrix products, arithmetic and copies ran while one was open for 0% -> 0% of each run, Pallas kernels for 1% -> 1%
where the time goes in v3:
time: 44.6 us; the launch traced here: 44 us
  starting transfers between devices  14.7 us (33%)
  waiting for transfers between devices  14.6 us (33%)
  local copies, waits for them, and re-layouts  7.74 us (17%)
  Pallas kernels  5.82 us (13%)
  other arithmetic  1.11 us (2%)
    ppermute x4, starting transfers between devices, shifted(): lax.ppermute(x, 'band', [(i, (i + by) % count) for i in range(count)])  14.7 us
    ppermute x4, waiting for transfers between devices, shifted(): lax.ppermute(x, 'band', [(i, (i + by) % count) for i in range(count)])  14.6 us
    unnamed x16, local copies, waits for them, and re-layouts  7.74 us
    pallas_call x1, Pallas kernels, exchange(): pl.pallas_call(functools.partial(exchange_kernel, steps), out_shape=[jax....  5.33 us
    broadcast_in_dim x1, other arithmetic, local(): return total[None]  1.11 us
  transfers between devices with their start and end apart: 4, of which 2 were waited for; matrix products, arithmetic and copies ran while one was open for 0% of the time, Pallas kernels for 1%

profile of v3, /device:TPU:4, one launch (start us, length us, event | category | flops | bytes accessed | tf_op | source)
XLA Modules:
  0.0 44.0 jit_solution(7887410366964751981)
XLA Ops:
  0.0 1.2 %collective-permute-start.1 = (bf16[2048,128]{1,0:T(8,128)(2,1)}, bf16[2048,128]{1,0:T(8,128)(2,1)S(1)}, u32[]{:S(2)}, u32[]{:S(2)}) collective-permute-start(bf16[2048,128]{1,0:T(8,128)(2,1)} %bitcast.3), channel_id=1, source_target_pairs={{0,1},{1,2},{2,3},{3,4},{4,5},{5,6},{6,7},{7,8},{8,9},{9,10},{10,1... | collective-permute-start | bytes 1572872 | tf_op jit(solution)/shard_map/ppermute | solution.py:199
  1.2 8.3 %collective-permute-start = (bf16[2048,128]{1,0:T(8,128)(2,1)}, bf16[2048,128]{1,0:T(8,128)(2,1)S(1)}, u32[]{:S(2)}, u32[]{:S(2)}) collective-permute-start(bf16[2048,128]{1,0:T(8,128)(2,1)} %bitcast.4), channel_id=1, source_target_pairs={{0,62},{1,63},{2,0},{3,1},{4,2},{5,3},{6,4},{7,5},{8,6},{9,7},{10,... | collective-permute-start | bytes 1572872 | tf_op jit(solution)/shard_map/ppermute | solution.py:199
  9.5 0.0 copy-start
  9.5 1.6 %copy-done = f32[4096,128]{1,0:T(8,128)S(1)} copy-done((f32[4096,128]{1,0:T(8,128)S(1)}, f32[4096,128]{1,0:T(8,128)}, u32[]{:S(2)}) %copy-start) | copy-done | bytes 2097176
  11.1 0.0 copy-start.1
  11.1 1.0 %copy-done.1 = bf16[1,2048,128]{2,1,0:T(8,128)(2,1)S(1)} copy-done((bf16[1,2048,128]{2,1,0:T(8,128)(2,1)S(1)}, bf16[1,2048,128]{2,1,0:T(8,128)(2,1)}, u32[]{:S(2)}) %copy-start.1) | copy-done | bytes 524312
  12.1 0.0 copy-start.2
  12.1 1.0 %copy-done.2 = bf16[512,512]{1,0:T(8,128)(2,1)S(1)} copy-done((bf16[512,512]{1,0:T(8,128)(2,1)S(1)}, bf16[512,512]{1,0:T(8,128)(2,1)}, u32[]{:S(2)}) %copy-start.2) | copy-done | bytes 524312
  13.2 0.0 copy-start.3
  13.2 1.0 %copy-done.3 = bf16[512,512]{1,0:T(8,128)(2,1)S(1)} copy-done((bf16[512,512]{1,0:T(8,128)(2,1)S(1)}, bf16[512,512]{1,0:T(8,128)(2,1)}, u32[]{:S(2)}) %copy-start.3) | copy-done | bytes 524312
  14.2 0.0 copy-start.4
  14.2 0.8 %copy-done.4 = bf16[128,128]{1,0:T(8,128)(2,1)S(1)} copy-done((bf16[128,128]{1,0:T(8,128)(2,1)S(1)}, bf16[128,128]{1,0:T(8,128)(2,1)}, u32[]{:S(2)}) %copy-start.4) | copy-done | bytes 32792
  15.0 0.0 copy-start.5
  15.0 0.8 %copy-done.5 = bf16[128,128]{1,0:T(8,128)(2,1)S(1)} copy-done((bf16[128,128]{1,0:T(8,128)(2,1)S(1)}, bf16[128,128]{1,0:T(8,128)(2,1)}, u32[]{:S(2)}) %copy-start.5) | copy-done | bytes 32792
  15.7 0.0 copy-start.6
  15.7 0.8 %copy-done.6 = bf16[128,128]{1,0:T(8,128)(2,1)S(1)} copy-done((bf16[128,128]{1,0:T(8,128)(2,1)S(1)}, bf16[128,128]{1,0:T(8,128)(2,1)}, u32[]{:S(2)}) %copy-start.6) | copy-done | bytes 32792
  16.5 0.0 copy-start.7
  16.5 0.8 %copy-done.7 = bf16[128,128]{1,0:T(8,128)(2,1)S(1)} copy-done((bf16[128,128]{1,0:T(8,128)(2,1)S(1)}, bf16[128,128]{1,0:T(8,128)(2,1)}, u32[]{:S(2)}) %copy-start.7) | copy-done | bytes 32792
  17.3 0.5 %shard_map.82 = (bf16[2048,128]{1,0:T(8,128)(2,1)S(1)}, bf16[512,512]{1,0:T(8,128)(2,1)S(1)}, bf16[128,128]{1,0:T(8,128)(2,1)S(1)}, bf16[128,128]{1,0:T(8,128)(2...) custom-call(bf16[2048,128]{1,0:T(8,128)(2,1)S(1)} %bitcast.5, ...), custom_call_target="tpu_custom_call" | custom-call | bytes 8388608 | tf_op jit(solution)/shard_map/pallas_call | solution.py:167
  17.8 3.3 %collective-permute-done.1.behind_ref = bf16[2048,128]{1,0:T(8,128)(2,1)S(1)} collective-permute-done((bf16[2048,128]{1,0:T(8,128)(2,1)}, bf16[2048,128]{1,0:T(8,128)(2,1)S(1)}, u32[]{:S(2)}, u32[]{:S(2)}) %collective-permute-start.1) | collective-permute-done | bytes 524320 | tf_op jit(solution)/shard_map/ppermute | solution.py:199
  21.1 0.0 collective-permute-done.ahead_ref
  21.1 5.3 %shard_map.83 = (f32[2048,128]{1,0:T(8,128)S(1)}, bf16[2048,128]{1,0:T(8,128)(2,1)S(1)}, bf16[2048,128]{1,0:T(8,128)(2,1)S(1)}) custom-call(bf16[2048,128]{1,0:T(8,128)(2,1)S(1)} %get-tuple-element.16.own_ref, bf16[2048,128]{1,0:T(8,128)(2,1)S(1)} %collective-permute-done.ahead_ref, bf16[2048,128]{1,0:T(8,128)(2,1)S(1)} %collective-permute-done.1.behind_ref, ...), custom_call_target="tpu_custom_call" | custom-call | flops 4294967296 | bytes 8388608 | tf_op jit(solution)/shard_map/pallas_call | solution.py:182
  26.4 0.1 collective-permute-start.2
  26.5 5.1 %collective-permute-start.3 = (bf16[2048,128]{1,0:T(8,128)(2,1)S(1)}, bf16[2048,128]{1,0:T(8,128)(2,1)S(1)}, u32[]{:S(2)}, u32[]{:S(2)}) collective-permute-start(bf16[2048,128]{1,0:T(8,128)(2,1)S(1)} %get-tuple-element.26), channel_id=1, source_target_pairs={{0,63},{1,0},{2,1},{3,2},{4,3},{5,4},{6,5},{7,6},{8,7},{9,8},{10,9... | collective-permute-start | bytes 1572872 | tf_op jit(solution)/shard_map/ppermute | solution.py:199
  31.6 11.3 %collective-permute-done.2 = bf16[2048,128]{1,0:T(8,128)(2,1)S(1)} collective-permute-done((bf16[2048,128]{1,0:T(8,128)(2,1)S(1)}, bf16[2048,128]{1,0:T(8,128)(2,1)S(1)}, u32[]{:S(2)}, u32[]{:S(2)}) %collective-permute-start.2) | collective-permute-done | bytes 524320 | tf_op jit(solution)/shard_map/ppermute | solution.py:199
  42.9 0.0 collective-permute-done.3
  42.9 1.1 %add_bitcast_fusion = f32[1,2048,128]{2,1,0:T(8,128)} fusion(bf16[2048,128]{1,0:T(8,128)(2,1)S(1)} %collective-permute-done.3, f32[2048,128]{1,0:T(8,128)S(1)} %get-tuple-element.24, bf16[2048,128]{1,0:T(8,128)(2,1)S(1)} %collective-permute-done.2), kind=kLoop, calls=%fused_computation | loop fusion | flops 1048576 | bytes 3145728 | tf_op jit(solution)/shard_map/broadcast_in_dim | solution.py:209
Async XLA Ops:
  0.0 21.1 %collective-permute-start.1 = (bf16[2048,128]{1,0:T(8,128)(2,1)}, bf16[2048,128]{1,0:T(8,128)(2,1)S(1)}, u32[]{:S(2)}, u32[]{:S(2)}) collective-permute-start(bf16[2048,128]{1,0:T(8,128)(2,1)} %bitcast.3), channel_id=1, source_target_pairs={{0,1},{1,2},{2,3},{3,4},{4,5},{5,6},{6,7},{7,8},{8,9},{9,10},{10,1... | collective-permute-start | bytes 1572872 | tf_op jit(solution)/shard_map/ppermute | solution.py:199
  1.2 19.9 %collective-permute-start = (bf16[2048,128]{1,0:T(8,128)(2,1)}, bf16[2048,128]{1,0:T(8,128)(2,1)S(1)}, u32[]{:S(2)}, u32[]{:S(2)}) collective-permute-start(bf16[2048,128]{1,0:T(8,128)(2,1)} %bitcast.4), channel_id=1, source_target_pairs={{0,62},{1,63},{2,0},{3,1},{4,2},{5,3},{6,4},{7,5},{8,6},{9,7},{10,... | collective-permute-start | bytes 1572872 | tf_op jit(solution)/shard_map/ppermute | solution.py:199
  9.5 1.6 %copy-start = (f32[4096,128]{1,0:T(8,128)S(1)}, f32[4096,128]{1,0:T(8,128)}, u32[]{:S(2)}) copy-start(f32[4096,128]{1,0:T(8,128)} %constant.17.clone.refs_4_) | copy-start | bytes 6291460
  11.1 1.0 %copy-start.1 = (bf16[1,2048,128]{2,1,0:T(8,128)(2,1)S(1)}, bf16[1,2048,128]{2,1,0:T(8,128)(2,1)}, u32[]{:S(2)}) copy-start(bf16[1,2048,128]{2,1,0:T(8,128)(2,1)} %param.8) | copy-start | bytes 1572868
  12.1 1.0 %copy-start.2 = (bf16[512,512]{1,0:T(8,128)(2,1)S(1)}, bf16[512,512]{1,0:T(8,128)(2,1)}, u32[]{:S(2)}) copy-start(bf16[512,512]{1,0:T(8,128)(2,1)} %constant.20.clone.refs_7_) | copy-start | bytes 1572868
  13.2 1.0 %copy-start.3 = (bf16[512,512]{1,0:T(8,128)(2,1)S(1)}, bf16[512,512]{1,0:T(8,128)(2,1)}, u32[]{:S(2)}) copy-start(bf16[512,512]{1,0:T(8,128)(2,1)} %constant.14.clone.refs_1_) | copy-start | bytes 1572868
  14.2 0.8 %copy-start.4 = (bf16[128,128]{1,0:T(8,128)(2,1)S(1)}, bf16[128,128]{1,0:T(8,128)(2,1)}, u32[]{:S(2)}) copy-start(bf16[128,128]{1,0:T(8,128)(2,1)} %constant.19.clone.refs_6_) | copy-start | bytes 98308
  15.0 0.8 %copy-start.5 = (bf16[128,128]{1,0:T(8,128)(2,1)S(1)}, bf16[128,128]{1,0:T(8,128)(2,1)}, u32[]{:S(2)}) copy-start(bf16[128,128]{1,0:T(8,128)(2,1)} %constant.18.clone.refs_5_) | copy-start | bytes 98308
  15.7 0.8 %copy-start.6 = (bf16[128,128]{1,0:T(8,128)(2,1)S(1)}, bf16[128,128]{1,0:T(8,128)(2,1)}, u32[]{:S(2)}) copy-start(bf16[128,128]{1,0:T(8,128)(2,1)} %constant.16.clone.refs_3_) | copy-start | bytes 98308
  16.5 0.8 %copy-start.7 = (bf16[128,128]{1,0:T(8,128)(2,1)S(1)}, bf16[128,128]{1,0:T(8,128)(2,1)}, u32[]{:S(2)}) copy-start(bf16[128,128]{1,0:T(8,128)(2,1)} %constant.15.clone.refs_2_) | copy-start | bytes 98308
  26.4 16.5 %collective-permute-start.2 = (bf16[2048,128]{1,0:T(8,128)(2,1)S(1)}, bf16[2048,128]{1,0:T(8,128)(2,1)S(1)}, u32[]{:S(2)}, u32[]{:S(2)}) collective-permute-start(bf16[2048,128]{1,0:T(8,128)(2,1)S(1)} %get-tuple-element.25), channel_id=1, source_target_pairs={{0,2},{1,3},{2,4},{3,5},{4,6},{5,7},{6,8},{7,9},{8,10},{9,11},{10,... | collective-permute-start | bytes 1572872 | tf_op jit(solution)/shard_map/ppermute | solution.py:199
  26.5 16.4 %collective-permute-start.3 = (bf16[2048,128]{1,0:T(8,128)(2,1)S(1)}, bf16[2048,128]{1,0:T(8,128)(2,1)S(1)}, u32[]{:S(2)}, u32[]{:S(2)}) collective-permute-start(bf16[2048,128]{1,0:T(8,128)(2,1)S(1)} %get-tuple-element.26), channel_id=1, source_target_pairs={{0,63},{1,0},{2,1},{3,2},{4,3},{5,4},{6,5},{7,6},{8,7},{9,8},{10,9... | collective-permute-start | bytes 1572872 | tf_op jit(solution)/shard_map/ppermute | solution.py:199

commit v4 on v3

--- a/solution.py
+++ b/solution.py
@@ -43,8 +43,11 @@
             for place, plane in ((even, 0), (even + 1, HALF)):
                 into[band, parity, :, parity, band % 2, place, 0] = cosine[:, plane]
                 back[parity, band % 2, place, 0, band, parity, :] = cosine[plane]
-    into = into.reshape(SLOTS * LANES, SLOTS * LANES)
-    back = back.reshape(SLOTS * LANES, SLOTS * LANES)
+    wide = 2 * LANES
+    into_low = into[:2, :, :, :, :, :2].reshape(wide, wide)
+    into_high = into[2:, :, :, :, ::-1, 2:].reshape(wide, wide)
+    back_low = back[:, :, :2, :, :2].reshape(wide, wide)
+    back_high = back[:, ::-1, 2:, :, 2:].reshape(wide, wide)
     order = np.arange(NG).reshape(HALF, 2).T
     y_in = np.concatenate([np.concatenate([order[b] + NG * c for c in range(2)]) for b in range(2)])
     forward = paired(cosine, sine, 1.0)
@@ -58,13 +61,15 @@
     kernel = np.where(squared > 0, strength / np.maximum(squared, 1).astype(np.float32), np.float32(0))
     as_bf = lambda table: table.astype(ml_dtypes.bfloat16)
     return (
-        as_bf(into),
+        as_bf(into_low),
+        as_bf(into_high),
         as_bf(forward[:, y_in]),
         as_bf(forward),
         kernel.reshape(NG * NG, LANES).astype(np.float32),
         as_bf(inverse),
         as_bf(inverse[y_in]),
-        as_bf(back * np.float32(-MIXING / NG**3)),
+        as_bf(back_low * np.float32(-MIXING / NG**3)),
+        as_bf(back_high * np.float32(-MIXING / NG**3)),
     )
 
 
@@ -73,7 +78,9 @@
 
 
 def exchange_kernel(steps, own_ref, ahead_ref, behind_ref, *refs):
-    into, y_fwd, x_fwd, kernel, x_inv, y_inv, back, out_ref, to_ahead, to_behind, planes, spec, flat = refs
+    into_low, into_high, y_fwd, x_fwd, kernel, x_inv, y_inv, back_low, back_high, *refs = refs
+    out_ref, to_ahead, to_behind, planes, spec, flat = refs
+    low = lax.broadcasted_iota(jnp.int32, (steps[0] * HALF, LANES), 1) < NG
     block, x_unroll = steps
     rows = block * HALF
     blocks = NG // block
@@ -86,8 +93,17 @@
         base = pl.multiple_of(at * rows, rows)
         own, ahead, behind = (wide(ref, base) for ref in (own_ref, ahead_ref, behind_ref))
         density = [own * own, own * ahead, behind * own, behind * ahead]
-        density = jnp.concatenate([d.astype(jnp.bfloat16) for d in density], axis=1)
-        flat[...] = dot(density, into[...]).astype(jnp.bfloat16)
+        density = [d.astype(jnp.bfloat16) for d in density]
+        first = dot(jnp.concatenate(density[:2], axis=1), into_low[...])
+        other = dot(jnp.concatenate(density[2:], axis=1), into_high[...])
+        for parity in range(2):
+            lanes = slice(parity * LANES, (parity + 1) * LANES)
+            one, two = (x[:, lanes].astype(jnp.bfloat16) for x in (first, other))
+            real = jnp.where(low, one, two)
+            imag = jnp.where(low, two, one)
+            imag = jnp.concatenate([imag[:, NG:], imag[:, :NG]], axis=1)
+            flat[:, 2 * parity * LANES : (2 * parity + 1) * LANES] = real
+            flat[:, (2 * parity + 1) * LANES : (2 * parity + 2) * LANES] = imag
         for pair in range(block // 2):
             section = []
             for x in (2 * pair, 2 * pair + 1):
@@ -140,13 +156,17 @@
             back_two = dot(y_inv[...], section).astype(jnp.bfloat16)
             for n in range(2):
                 row = (2 * pair + n) * HALF
-                for t in range(4):
-                    flat[row : row + HALF, t * LANES : (t + 1) * LANES] = back_two[
-                        t * HALF : (t + 1) * HALF, n * LANES : (n + 1) * LANES
-                    ]
+                for parity in range(2):
+                    lanes = slice(n * LANES, (n + 1) * LANES)
+                    real = back_two[2 * parity * HALF : (2 * parity + 1) * HALF, lanes]
+                    imag = back_two[(2 * parity + 1) * HALF : (2 * parity + 2) * HALF, lanes]
+                    imag = jnp.concatenate([imag[:, NG:], imag[:, :NG]], axis=1)
+                    for half, pick in enumerate((jnp.where(low[:HALF], real, imag), jnp.where(low[:HALF], imag, real))):
+                        place = (2 * half + parity) * LANES
+                        flat[row : row + HALF, place : place + LANES] = pick
         base = pl.multiple_of(at * rows, rows)
-        field = dot(flat[...], back[...])
-        alone, onward, rearward, across = (field[:, p * LANES : (p + 1) * LANES] for p in range(SLOTS))
+        alone, onward = jnp.split(dot(flat[:, : 2 * LANES], back_low[...]), 2, axis=1)
+        rearward, across = jnp.split(dot(flat[:, 2 * LANES :], back_high[...]), 2, axis=1)
         own, ahead, behind = (wide(ref, base) for ref in (own_ref, ahead_ref, behind_ref))
         to_ahead[pl.ds(base, rows), :] = (own * onward + behind * across).astype(jnp.bfloat16)
         to_behind[pl.ds(base, rows), :] = (own * rearward + ahead * across).astype(jnp.bfloat16)
@@ -175,7 +195,7 @@
     )(*arrays)
 
 
-def exchange(own, ahead, behind, steps=(32, 32)):
+def exchange(own, ahead, behind, steps=(64, 32)):
     tables = [jnp.asarray(t) for t in make_tables()]
     own, *tables = held_in_vmem([own, *tables])
     operands = [own, ahead, behind, *tables]

time: 44.6 us -> 43.2 us (0.969)
  waiting for transfers between devices: 14.6 us -> 12.3 us
  local copies, waits for them, and re-layouts: 7.74 us -> 9.28 us
  Pallas kernels: 5.82 us -> 5.22 us
    ppermute x4, waiting for transfers between devices: 14.6 us -> 12.3 us  [shifted(): lax.ppermute(x, 'band', [(i, (i + by) % count) for i in range(count)])]
    unnamed x16 -> x20, local copies, waits for them, and re-layouts: 7.74 us -> 9.28 us
    pallas_call x1, Pallas kernels: 5.33 us -> 3.99 us  [exchange(): pl.pallas_call(functools.partial(exchange_kernel, steps), out_shape=[jax....]
    pallas_call x1, Pallas kernels: 0.49 us -> 1.23 us  [held_in_vmem(): pl.pallas_call(hold_kernel, out_shape=[pltpu.VMEM(x.shape, x.dtype) for x...]
  transfers between devices with their start and end apart: 4 -> 4, of which waited for: 2 -> 2; matrix products, arithmetic and copies ran while one was open for 0% -> 0% of each run, Pallas kernels for 1% -> 3%
where the time goes in v4:
time: 43.2 us; the launch traced here: 42.7 us
  starting transfers between devices  14.7 us (34%)
  waiting for transfers between devices  12.3 us (28%)
  local copies, waits for them, and re-layouts  9.28 us (21%)
  Pallas kernels  5.22 us (12%)
  other arithmetic  1.11 us (3%)
    ppermute x4, starting transfers between devices, shifted(): lax.ppermute(x, 'band', [(i, (i + by) % count) for i in range(count)])  14.7 us
    ppermute x4, waiting for transfers between devices, shifted(): lax.ppermute(x, 'band', [(i, (i + by) % count) for i in range(count)])  12.3 us
    unnamed x20, local copies, waits for them, and re-layouts  9.28 us
    pallas_call x1, Pallas kernels, exchange(): pl.pallas_call(functools.partial(exchange_kernel, steps), out_shape=[jax....  3.99 us
    pallas_call x1, Pallas kernels, held_in_vmem(): pl.pallas_call(hold_kernel, out_shape=[pltpu.VMEM(x.shape, x.dtype) for x...  1.23 us
    broadcast_in_dim x1, other arithmetic, local(): return total[None]  1.11 us
  transfers between devices with their start and end apart: 4, of which 2 were waited for; matrix products, arithmetic and copies ran while one was open for 0% of the time, Pallas kernels for 3%

profile of v4, /device:TPU:4, one launch (start us, length us, event | category | flops | bytes accessed | tf_op | source)
XLA Modules:
  0.0 42.7 jit_solution(9800538026028157868)
XLA Ops:
  0.0 1.2 %collective-permute-start.1 = (bf16[2048,128]{1,0:T(8,128)(2,1)}, bf16[2048,128]{1,0:T(8,128)(2,1)S(1)}, u32[]{:S(2)}, u32[]{:S(2)}) collective-permute-start(bf16[2048,128]{1,0:T(8,128)(2,1)} %bitcast.3), channel_id=1, source_target_pairs={{0,1},{1,2},{2,3},{3,4},{4,5},{5,6},{6,7},{7,8},{8,9},{9,10},{10,1... | collective-permute-start | bytes 1572872 | tf_op jit(solution)/shard_map/ppermute | solution.py:219
  1.2 8.3 %collective-permute-start = (bf16[2048,128]{1,0:T(8,128)(2,1)}, bf16[2048,128]{1,0:T(8,128)(2,1)S(1)}, u32[]{:S(2)}, u32[]{:S(2)}) collective-permute-start(bf16[2048,128]{1,0:T(8,128)(2,1)} %bitcast.4), channel_id=1, source_target_pairs={{0,62},{1,63},{2,0},{3,1},{4,2},{5,3},{6,4},{7,5},{8,6},{9,7},{10,... | collective-permute-start | bytes 1572872 | tf_op jit(solution)/shard_map/ppermute | solution.py:219
  9.5 0.0 copy-start
  9.5 1.6 %copy-done = f32[4096,128]{1,0:T(8,128)S(1)} copy-done((f32[4096,128]{1,0:T(8,128)S(1)}, f32[4096,128]{1,0:T(8,128)}, u32[]{:S(2)}) %copy-start) | copy-done | bytes 2097176
  11.1 0.0 copy-start.1
  11.1 1.0 %copy-done.1 = bf16[1,2048,128]{2,1,0:T(8,128)(2,1)S(1)} copy-done((bf16[1,2048,128]{2,1,0:T(8,128)(2,1)S(1)}, bf16[1,2048,128]{2,1,0:T(8,128)(2,1)}, u32[]{:S(2)}) %copy-start.1) | copy-done | bytes 524312
  12.1 0.0 copy-start.2
  12.1 0.9 %copy-done.2 = bf16[256,256]{1,0:T(8,128)(2,1)S(1)} copy-done((bf16[256,256]{1,0:T(8,128)(2,1)S(1)}, bf16[256,256]{1,0:T(8,128)(2,1)}, u32[]{:S(2)}) %copy-start.2) | copy-done | bytes 131096
  13.0 0.0 copy-start.3
  13.0 0.9 %copy-done.3 = bf16[256,256]{1,0:T(8,128)(2,1)S(1)} copy-done((bf16[256,256]{1,0:T(8,128)(2,1)S(1)}, bf16[256,256]{1,0:T(8,128)(2,1)}, u32[]{:S(2)}) %copy-start.3) | copy-done | bytes 131096
  13.9 0.0 copy-start.4
  14.0 0.9 %copy-done.4 = bf16[256,256]{1,0:T(8,128)(2,1)S(1)} copy-done((bf16[256,256]{1,0:T(8,128)(2,1)S(1)}, bf16[256,256]{1,0:T(8,128)(2,1)}, u32[]{:S(2)}) %copy-start.4) | copy-done | bytes 131096
  14.9 0.0 copy-start.5
  14.9 0.9 %copy-done.5 = bf16[256,256]{1,0:T(8,128)(2,1)S(1)} copy-done((bf16[256,256]{1,0:T(8,128)(2,1)S(1)}, bf16[256,256]{1,0:T(8,128)(2,1)}, u32[]{:S(2)}) %copy-start.5) | copy-done | bytes 131096
  15.8 0.0 copy-start.6
  15.8 0.8 %copy-done.6 = bf16[128,128]{1,0:T(8,128)(2,1)S(1)} copy-done((bf16[128,128]{1,0:T(8,128)(2,1)S(1)}, bf16[128,128]{1,0:T(8,128)(2,1)}, u32[]{:S(2)}) %copy-start.6) | copy-done | bytes 32792
  16.5 0.0 copy-start.7
  16.5 0.8 %copy-done.7 = bf16[128,128]{1,0:T(8,128)(2,1)S(1)} copy-done((bf16[128,128]{1,0:T(8,128)(2,1)S(1)}, bf16[128,128]{1,0:T(8,128)(2,1)}, u32[]{:S(2)}) %copy-start.7) | copy-done | bytes 32792
  17.3 0.0 copy-start.8
  17.3 0.8 %copy-done.8 = bf16[128,128]{1,0:T(8,128)(2,1)S(1)} copy-done((bf16[128,128]{1,0:T(8,128)(2,1)S(1)}, bf16[128,128]{1,0:T(8,128)(2,1)}, u32[]{:S(2)}) %copy-start.8) | copy-done | bytes 32792
  18.0 0.0 copy-start.9
  18.0 0.8 %copy-done.9 = bf16[128,128]{1,0:T(8,128)(2,1)S(1)} copy-done((bf16[128,128]{1,0:T(8,128)(2,1)S(1)}, bf16[128,128]{1,0:T(8,128)(2,1)}, u32[]{:S(2)}) %copy-start.9) | copy-done | bytes 32792
  18.8 1.2 %shard_map.100 = (bf16[2048,128]{1,0:T(8,128)(2,1)S(1)}, bf16[256,256]{1,0:T(8,128)(2,1)S(1)}, bf16[256,256]{1,0:T(8,128)(2,1)S(1)}, bf16[128,128]{1,0:T(8,128)(...) custom-call(bf16[2048,128]{1,0:T(8,128)(2,1)S(1)} %bitcast.5, ...), custom_call_target="tpu_custom_call" | custom-call | bytes 8388608 | tf_op jit(solution)/shard_map/pallas_call | solution.py:187
  20.0 1.0 %collective-permute-done.1.behind_ref = bf16[2048,128]{1,0:T(8,128)(2,1)S(1)} collective-permute-done((bf16[2048,128]{1,0:T(8,128)(2,1)}, bf16[2048,128]{1,0:T(8,128)(2,1)S(1)}, u32[]{:S(2)}, u32[]{:S(2)}) %collective-permute-start.1) | collective-permute-done | bytes 524320 | tf_op jit(solution)/shard_map/ppermute | solution.py:219
  21.1 0.0 collective-permute-done.ahead_ref
  21.1 4.0 %shard_map.101 = (f32[2048,128]{1,0:T(8,128)S(1)}, bf16[2048,128]{1,0:T(8,128)(2,1)S(1)}, bf16[2048,128]{1,0:T(8,128)(2,1)S(1)}) custom-call(bf16[2048,128]{1,0:T(8,128)(2,1)S(1)} %get-tuple-element.18.own_ref, bf16[2048,128]{1,0:T(8,128)(2,1)S(1)} %collective-permute-done.ahead_ref, bf16[2048,128]{1,0:T(8,128)(2,1)S(1)} %collective-permute-done.1.behind_ref, ...), custom_call_target="tpu_custom_call" | custom-call | flops 4294967296 | bytes 8388608 | tf_op jit(solution)/shard_map/pallas_call | solution.py:202
  25.1 0.1 collective-permute-start.2
  25.2 5.1 %collective-permute-start.3 = (bf16[2048,128]{1,0:T(8,128)(2,1)S(1)}, bf16[2048,128]{1,0:T(8,128)(2,1)S(1)}, u32[]{:S(2)}, u32[]{:S(2)}) collective-permute-start(bf16[2048,128]{1,0:T(8,128)(2,1)S(1)} %get-tuple-element.30), channel_id=1, source_target_pairs={{0,63},{1,0},{2,1},{3,2},{4,3},{5,4},{6,5},{7,6},{8,7},{9,8},{10,9... | collective-permute-start | bytes 1572872 | tf_op jit(solution)/shard_map/ppermute | solution.py:219
  30.3 11.3 %collective-permute-done.2 = bf16[2048,128]{1,0:T(8,128)(2,1)S(1)} collective-permute-done((bf16[2048,128]{1,0:T(8,128)(2,1)S(1)}, bf16[2048,128]{1,0:T(8,128)(2,1)S(1)}, u32[]{:S(2)}, u32[]{:S(2)}) %collective-permute-start.2) | collective-permute-done | bytes 524320 | tf_op jit(solution)/shard_map/ppermute | solution.py:219
  41.6 0.0 collective-permute-done.3
  41.6 1.1 %add_bitcast_fusion = f32[1,2048,128]{2,1,0:T(8,128)} fusion(bf16[2048,128]{1,0:T(8,128)(2,1)S(1)} %collective-permute-done.3, f32[2048,128]{1,0:T(8,128)S(1)} %get-tuple-element.28, bf16[2048,128]{1,0:T(8,128)(2,1)S(1)} %collective-permute-done.2), kind=kLoop, calls=%fused_computation | loop fusion | flops 1048576 | bytes 3145728 | tf_op jit(solution)/shard_map/broadcast_in_dim | solution.py:229
Async XLA Ops:
  0.0 21.1 %collective-permute-start.1 = (bf16[2048,128]{1,0:T(8,128)(2,1)}, bf16[2048,128]{1,0:T(8,128)(2,1)S(1)}, u32[]{:S(2)}, u32[]{:S(2)}) collective-permute-start(bf16[2048,128]{1,0:T(8,128)(2,1)} %bitcast.3), channel_id=1, source_target_pairs={{0,1},{1,2},{2,3},{3,4},{4,5},{5,6},{6,7},{7,8},{8,9},{9,10},{10,1... | collective-permute-start | bytes 1572872 | tf_op jit(solution)/shard_map/ppermute | solution.py:219
  1.2 19.9 %collective-permute-start = (bf16[2048,128]{1,0:T(8,128)(2,1)}, bf16[2048,128]{1,0:T(8,128)(2,1)S(1)}, u32[]{:S(2)}, u32[]{:S(2)}) collective-permute-start(bf16[2048,128]{1,0:T(8,128)(2,1)} %bitcast.4), channel_id=1, source_target_pairs={{0,62},{1,63},{2,0},{3,1},{4,2},{5,3},{6,4},{7,5},{8,6},{9,7},{10,... | collective-permute-start | bytes 1572872 | tf_op jit(solution)/shard_map/ppermute | solution.py:219
  9.5 1.6 %copy-start = (f32[4096,128]{1,0:T(8,128)S(1)}, f32[4096,128]{1,0:T(8,128)}, u32[]{:S(2)}) copy-start(f32[4096,128]{1,0:T(8,128)} %constant.22.clone.refs_5_) | copy-start | bytes 6291460
  11.1 1.0 %copy-start.1 = (bf16[1,2048,128]{2,1,0:T(8,128)(2,1)S(1)}, bf16[1,2048,128]{2,1,0:T(8,128)(2,1)}, u32[]{:S(2)}) copy-start(bf16[1,2048,128]{2,1,0:T(8,128)(2,1)} %param.10) | copy-start | bytes 1572868
  12.1 0.9 %copy-start.2 = (bf16[256,256]{1,0:T(8,128)(2,1)S(1)}, bf16[256,256]{1,0:T(8,128)(2,1)}, u32[]{:S(2)}) copy-start(bf16[256,256]{1,0:T(8,128)(2,1)} %constant.26.clone.refs_9_) | copy-start | bytes 393220
  13.0 0.9 %copy-start.3 = (bf16[256,256]{1,0:T(8,128)(2,1)S(1)}, bf16[256,256]{1,0:T(8,128)(2,1)}, u32[]{:S(2)}) copy-start(bf16[256,256]{1,0:T(8,128)(2,1)} %constant.25.clone.refs_8_) | copy-start | bytes 393220
  13.9 0.9 %copy-start.4 = (bf16[256,256]{1,0:T(8,128)(2,1)S(1)}, bf16[256,256]{1,0:T(8,128)(2,1)}, u32[]{:S(2)}) copy-start(bf16[256,256]{1,0:T(8,128)(2,1)} %constant.19.clone.refs_2_) | copy-start | bytes 393220
  14.9 0.9 %copy-start.5 = (bf16[256,256]{1,0:T(8,128)(2,1)S(1)}, bf16[256,256]{1,0:T(8,128)(2,1)}, u32[]{:S(2)}) copy-start(bf16[256,256]{1,0:T(8,128)(2,1)} %constant.18.clone.refs_1_) | copy-start | bytes 393220
  15.8 0.8 %copy-start.6 = (bf16[128,128]{1,0:T(8,128)(2,1)S(1)}, bf16[128,128]{1,0:T(8,128)(2,1)}, u32[]{:S(2)}) copy-start(bf16[128,128]{1,0:T(8,128)(2,1)} %constant.24.clone.refs_7_) | copy-start | bytes 98308
  16.5 0.8 %copy-start.7 = (bf16[128,128]{1,0:T(8,128)(2,1)S(1)}, bf16[128,128]{1,0:T(8,128)(2,1)}, u32[]{:S(2)}) copy-start(bf16[128,128]{1,0:T(8,128)(2,1)} %constant.23.clone.refs_6_) | copy-start | bytes 98308
  17.3 0.8 %copy-start.8 = (bf16[128,128]{1,0:T(8,128)(2,1)S(1)}, bf16[128,128]{1,0:T(8,128)(2,1)}, u32[]{:S(2)}) copy-start(bf16[128,128]{1,0:T(8,128)(2,1)} %constant.21.clone.refs_4_) | copy-start | bytes 98308
  18.0 0.8 %copy-start.9 = (bf16[128,128]{1,0:T(8,128)(2,1)S(1)}, bf16[128,128]{1,0:T(8,128)(2,1)}, u32[]{:S(2)}) copy-start(bf16[128,128]{1,0:T(8,128)(2,1)} %constant.20.clone.refs_3_) | copy-start | bytes 98308
  25.1 16.5 %collective-permute-start.2 = (bf16[2048,128]{1,0:T(8,128)(2,1)S(1)}, bf16[2048,128]{1,0:T(8,128)(2,1)S(1)}, u32[]{:S(2)}, u32[]{:S(2)}) collective-permute-start(bf16[2048,128]{1,0:T(8,128)(2,1)S(1)} %get-tuple-element.29), channel_id=1, source_target_pairs={{0,2},{1,3},{2,4},{3,5},{4,6},{5,7},{6,8},{7,9},{8,10},{9,11},{10,... | collective-permute-start | bytes 1572872 | tf_op jit(solution)/shard_map/ppermute | solution.py:219
  25.2 16.4 %collective-permute-start.3 = (bf16[2048,128]{1,0:T(8,128)(2,1)S(1)}, bf16[2048,128]{1,0:T(8,128)(2,1)S(1)}, u32[]{:S(2)}, u32[]{:S(2)}) collective-permute-start(bf16[2048,128]{1,0:T(8,128)(2,1)S(1)} %get-tuple-element.30), channel_id=1, source_target_pairs={{0,63},{1,0},{2,1},{3,2},{4,3},{5,4},{6,5},{7,6},{8,7},{9,8},{10,9... | collective-permute-start | bytes 1572872 | tf_op jit(solution)/shard_map/ppermute | solution.py:219

commit v5 on v4

--- a/solution.py
+++ b/solution.py
@@ -15,6 +15,8 @@
 LANES = 128
 SLOTS = 4
 PITCH = 129
+ROWS = 64 * PITCH + LANES
+PARTS = 2
 MIXING = 0.25
 
 
@@ -77,18 +79,15 @@
     return jnp.dot(left, right, preferred_element_type=jnp.float32)
 
 
-def exchange_kernel(steps, own_ref, ahead_ref, behind_ref, *refs):
-    into_low, into_high, y_fwd, x_fwd, kernel, x_inv, y_inv, back_low, back_high, *refs = refs
-    out_ref, to_ahead, to_behind, planes, spec, flat = refs
-    low = lax.broadcasted_iota(jnp.int32, (steps[0] * HALF, LANES), 1) < NG
-    block, x_unroll = steps
+def forward_stages(own_ref, ahead_ref, behind_ref, into_low, into_high, y_fwd, x_fwd, kernel, x_inv, planes, spec, flat):
+    block, x_unroll = NG, HALF
     rows = block * HALF
-    blocks = NG // block
+    low = lax.broadcasted_iota(jnp.int32, (rows, LANES), 1) < NG
 
     def wide(ref, base):
         return ref[pl.ds(base, rows), :].astype(jnp.float32)
 
-    @pl.loop(0, blocks)
+    @pl.loop(0, 1)
     def _(at):
         base = pl.multiple_of(at * rows, rows)
         own, ahead, behind = (wide(ref, base) for ref in (own_ref, ahead_ref, behind_ref))
@@ -140,7 +139,17 @@
             for n in range(2):
                 spec[pl.ds((ky + n) * PITCH, LANES), :] = back_one[:, n * LANES : (n + 1) * LANES]
 
-    @pl.loop(0, blocks)
+
+def last_stages(part, parts, own_ref, ahead_ref, behind_ref, y_inv, back_low, back_high, spec, outputs, flat):
+    out_ref, to_ahead, to_behind = outputs
+    block = NG // parts
+    rows = block * HALF
+    low = lax.broadcasted_iota(jnp.int32, (rows, LANES), 1) < NG
+
+    def wide(ref, base):
+        return ref[pl.ds(base, rows), :].astype(jnp.float32)
+
+    @pl.loop(part, part + 1)
     def _(at):
         for pair in range(block // 2):
             x = at * block + 2 * pair
@@ -165,12 +174,43 @@
                         place = (2 * half + parity) * LANES
                         flat[row : row + HALF, place : place + LANES] = pick
         base = pl.multiple_of(at * rows, rows)
-        alone, onward = jnp.split(dot(flat[:, : 2 * LANES], back_low[...]), 2, axis=1)
-        rearward, across = jnp.split(dot(flat[:, 2 * LANES :], back_high[...]), 2, axis=1)
+        alone, onward = jnp.split(dot(flat[:rows, : 2 * LANES], back_low[...]), 2, axis=1)
+        rearward, across = jnp.split(dot(flat[:rows, 2 * LANES :], back_high[...]), 2, axis=1)
         own, ahead, behind = (wide(ref, base) for ref in (own_ref, ahead_ref, behind_ref))
-        to_ahead[pl.ds(base, rows), :] = (own * onward + behind * across).astype(jnp.bfloat16)
-        to_behind[pl.ds(base, rows), :] = (own * rearward + ahead * across).astype(jnp.bfloat16)
-        out_ref[pl.ds(base, rows), :] = own * alone + ahead * onward + behind * rearward
+        to_ahead[...] = (own * onward + behind * across).astype(jnp.bfloat16)
+        to_behind[...] = (own * rearward + ahead * across).astype(jnp.bfloat16)
+        out_ref[...] = own * alone + ahead * onward + behind * rearward
+
+
+def first_kernel(*refs):
+    orbitals, refs = refs[:3], refs[3:]
+    into_low, into_high, y_fwd, x_fwd, kernel, x_inv, y_inv, back_low, back_high, *refs = refs
+    *outputs, spec, planes, flat = refs
+    forward_stages(*orbitals, into_low, into_high, y_fwd, x_fwd, kernel, x_inv, planes, spec, flat)
+    last_stages(0, PARTS, *orbitals, y_inv, back_low, back_high, spec, outputs, flat)
+
+
+def second_kernel(part, *refs):
+    orbitals, refs = refs[:3], refs[3:]
+    y_inv, back_low, back_high, spec, *refs = refs
+    *outputs, flat = refs
+    last_stages(part, PARTS, *orbitals, y_inv, back_low, back_high, spec, outputs, flat)
+
+
+def finish_kernel(*refs):
+    groups, out_ref, held, sem = refs[:-3], refs[-3], refs[-2], refs[-1]
+    rows = groups[0].shape[0]
+    copies = []
+    for n in range(len(groups) // 3):
+        total, one, two = groups[3 * n : 3 * n + 3]
+        for half in range(2):
+            here = pl.ds(half * (rows // 2), rows // 2)
+            there = pl.ds(n * rows + half * (rows // 2), rows // 2)
+            held[there, :] = total[here, :] + one[here, :].astype(jnp.float32) + two[here, :].astype(jnp.float32)
+            copies.append(pltpu.make_async_copy(held.at[there], out_ref.at[there], sem.at[2 * n + half]))
+            copies[-1].start()
+    for copy in copies:
+        copy.wait()
 
 
 def hold_kernel(*refs):
@@ -195,22 +235,28 @@
     )(*arrays)
 
 
-def exchange(own, ahead, behind, steps=(64, 32)):
-    tables = [jnp.asarray(t) for t in make_tables()]
-    own, *tables = held_in_vmem([own, *tables])
-    operands = [own, ahead, behind, *tables]
+def vmem_call(kernel, outputs, scratch, operands, flops):
     return pl.pallas_call(
-        functools.partial(exchange_kernel, steps),
-        out_shape=[jax.ShapeDtypeStruct(own.shape, t) for t in (jnp.float32, jnp.bfloat16, jnp.bfloat16)],
+        kernel,
+        out_shape=outputs,
         in_specs=[pl.BlockSpec(memory_space=pltpu.VMEM)] * len(operands),
-        out_specs=[pl.BlockSpec(memory_space=pltpu.VMEM)] * 3,
-        scratch_shapes=[
-            pltpu.VMEM((NG * PITCH, LANES), jnp.float32),
-            pltpu.VMEM((NG * PITCH, LANES), jnp.float32),
-            pltpu.VMEM((steps[0] * HALF, SLOTS * LANES), jnp.bfloat16),
-        ],
+        out_specs=[pl.BlockSpec(memory_space=pltpu.VMEM)] * len(outputs),
+        scratch_shapes=scratch,
         compiler_params=pltpu.CompilerParams(vmem_limit_bytes=24 * 1024 * 1024),
-        cost_estimate=pl.CostEstimate(flops=2**32, bytes_accessed=8 << 20, transcendentals=0),
+        cost_estimate=pl.CostEstimate(flops=flops, bytes_accessed=8 << 20, transcendentals=0),
+    )(*operands)
+
+
+def finished(groups, rows):
+    operands = [x for group in groups for x in group]
+    return pl.pallas_call(
+        finish_kernel,
+        out_shape=jax.ShapeDtypeStruct((rows, LANES), jnp.float32),
+        in_specs=[pl.BlockSpec(memory_space=pltpu.VMEM)] * len(operands),
+        out_specs=pl.BlockSpec(memory_space=pl.ANY),
+        scratch_shapes=[pltpu.VMEM((rows, LANES), jnp.float32), pltpu.SemaphoreType.DMA((2 * len(groups),))],
+        compiler_params=pltpu.CompilerParams(vmem_limit_bytes=16 * 1024 * 1024),
+        cost_estimate=pl.CostEstimate(flops=2**20, bytes_accessed=3 << 20, transcendentals=0),
     )(*operands)
 
 
@@ -220,13 +266,22 @@
 
 
 def local(orbitals):
-    own = orbitals[0]
-    behind = shifted(own, 1)
-    ahead = shifted(own, -2)
-    total, to_ahead, to_behind = exchange(own, ahead, behind)
-    total = total + shifted(to_ahead, 2).astype(jnp.float32)
-    total = total + shifted(to_behind, -1).astype(jnp.float32)
-    return total[None]
+    rows = orbitals.shape[1]
+    behind = shifted(orbitals[0], 1)
+    ahead = shifted(orbitals[0], -2)
+    own, *tables = held_in_vmem([orbitals[0], *(jnp.asarray(t) for t in make_tables())])
+    part = [pltpu.VMEM((rows // PARTS, LANES), t) for t in (jnp.float32, jnp.bfloat16, jnp.bfloat16)]
+    planes = pltpu.VMEM((ROWS, LANES), jnp.float32)
+    scratch = [planes, pltpu.VMEM((rows, SLOTS * LANES), jnp.bfloat16)]
+    *terms, spec = vmem_call(first_kernel, part + [planes], scratch, [own, ahead, behind, *tables], 2**32)
+    groups = []
+    for n in range(PARTS):
+        if n > 0:
+            operands = [own, ahead, behind, *tables[-3:], spec]
+            terms = vmem_call(functools.partial(second_kernel, n), part, scratch[1:], operands, 2**30)
+        total, to_ahead, to_behind = terms
+        groups.append([total, shifted(to_ahead, 2), shifted(to_behind, -1)])
+    return finished(groups, rows)[None]
 
 
 def solution(mesh):

time: 43.2 us -> 42.6 us (0.986)
  waiting for transfers between devices: 12.3 us -> 9.68 us
  starting transfers between devices: 14.7 us -> 16.6 us
  Pallas kernels: 5.22 us -> 6.43 us
  other arithmetic: 1.11 us -> 0 us
    ppermute x4 -> x6, waiting for transfers between devices: 12.3 us -> 9.68 us  [shifted(): lax.ppermute(x, 'band', [(i, (i + by) % count) for i in range(count)])]
    ppermute x4 -> x6, starting transfers between devices: 14.7 us -> 16.6 us  [shifted(): lax.ppermute(x, 'band', [(i, (i + by) % count) for i in range(count)])]
    pallas_call x1 -> x3, Pallas kernels: 3.99 us -> 5.2 us  [the longest x2 4.17 us: vmem_call(): pl.pallas_call(kernel, out_shape=outputs, in_specs=[pl.BlockSpec(memory_s...]
    broadcast_in_dim x1 -> x0, other arithmetic: 1.11 us -> none  [local(): return total[None]]
  transfers between devices with their start and end apart: 4 -> 6, of which waited for: 2 -> 4; matrix products, arithmetic and copies ran while one was open for 0% -> 0% of each run, Pallas kernels for 3% -> 5%
where the time goes in v5:
time: 42.6 us; the launch traced here: 42.1 us
  starting transfers between devices  16.6 us (39%)
  waiting for transfers between devices  9.68 us (23%)
  local copies, waits for them, and re-layouts  9.28 us (22%)
  Pallas kernels  6.43 us (15%)
    ppermute x6, starting transfers between devices, shifted(): lax.ppermute(x, 'band', [(i, (i + by) % count) for i in range(count)])  16.6 us
    ppermute x6, waiting for transfers between devices, shifted(): lax.ppermute(x, 'band', [(i, (i + by) % count) for i in range(count)])  9.68 us
    unnamed x20, local copies, waits for them, and re-layouts  9.28 us
    pallas_call x2, Pallas kernels, vmem_call(): pl.pallas_call(kernel, out_shape=outputs, in_specs=[pl.BlockSpec(memory_s...  4.17 us
    pallas_call x1, Pallas kernels, held_in_vmem(): pl.pallas_call(hold_kernel, out_shape=[pltpu.VMEM(x.shape, x.dtype) for x...  1.23 us
    pallas_call x1, Pallas kernels, finished(): pl.pallas_call(finish_kernel, out_shape=jax.ShapeDtypeStruct((rows, LANES...  1.03 us
  transfers between devices with their start and end apart: 6, of which 4 were waited for; matrix products, arithmetic and copies ran while one was open for 0% of the time, Pallas kernels for 5%

profile of v5, /device:TPU:4, one launch (start us, length us, event | category | flops | bytes accessed | tf_op | source)
XLA Modules:
  0.0 42.1 jit_solution(16716321137509853541)
XLA Ops:
  0.0 1.2 %collective-permute-start.1 = (bf16[2048,128]{1,0:T(8,128)(2,1)}, bf16[2048,128]{1,0:T(8,128)(2,1)S(1)}, u32[]{:S(2)}, u32[]{:S(2)}) collective-permute-start(bf16[2048,128]{1,0:T(8,128)(2,1)} %bitcast.2), channel_id=1, source_target_pairs={{0,1},{1,2},{2,3},{3,4},{4,5},{5,6},{6,7},{7,8},{8,9},{9,10},{10,1... | collective-permute-start | bytes 1572872 | tf_op jit(solution)/shard_map/ppermute | solution.py:265
  1.2 8.3 %collective-permute-start = (bf16[2048,128]{1,0:T(8,128)(2,1)}, bf16[2048,128]{1,0:T(8,128)(2,1)S(1)}, u32[]{:S(2)}, u32[]{:S(2)}) collective-permute-start(bf16[2048,128]{1,0:T(8,128)(2,1)} %bitcast.3), channel_id=1, source_target_pairs={{0,62},{1,63},{2,0},{3,1},{4,2},{5,3},{6,4},{7,5},{8,6},{9,7},{10,... | collective-permute-start | bytes 1572872 | tf_op jit(solution)/shard_map/ppermute | solution.py:265
  9.5 0.0 copy-start
  9.5 1.6 %copy-done = f32[4096,128]{1,0:T(8,128)S(1)} copy-done((f32[4096,128]{1,0:T(8,128)S(1)}, f32[4096,128]{1,0:T(8,128)}, u32[]{:S(2)}) %copy-start) | copy-done | bytes 2097176
  11.1 0.0 copy-start.1
  11.1 1.0 %copy-done.1 = bf16[1,2048,128]{2,1,0:T(8,128)(2,1)S(1)} copy-done((bf16[1,2048,128]{2,1,0:T(8,128)(2,1)S(1)}, bf16[1,2048,128]{2,1,0:T(8,128)(2,1)}, u32[]{:S(2)}) %copy-start.1) | copy-done | bytes 524312
  12.1 0.0 copy-start.2
  12.1 0.9 %copy-done.2 = bf16[256,256]{1,0:T(8,128)(2,1)S(1)} copy-done((bf16[256,256]{1,0:T(8,128)(2,1)S(1)}, bf16[256,256]{1,0:T(8,128)(2,1)}, u32[]{:S(2)}) %copy-start.2) | copy-done | bytes 131096
  13.0 0.0 copy-start.3
  13.0 0.9 %copy-done.3 = bf16[256,256]{1,0:T(8,128)(2,1)S(1)} copy-done((bf16[256,256]{1,0:T(8,128)(2,1)S(1)}, bf16[256,256]{1,0:T(8,128)(2,1)}, u32[]{:S(2)}) %copy-start.3) | copy-done | bytes 131096
  13.9 0.0 copy-start.4
  14.0 0.9 %copy-done.4 = bf16[256,256]{1,0:T(8,128)(2,1)S(1)} copy-done((bf16[256,256]{1,0:T(8,128)(2,1)S(1)}, bf16[256,256]{1,0:T(8,128)(2,1)}, u32[]{:S(2)}) %copy-start.4) | copy-done | bytes 131096
  14.9 0.0 copy-start.5
  14.9 0.9 %copy-done.5 = bf16[256,256]{1,0:T(8,128)(2,1)S(1)} copy-done((bf16[256,256]{1,0:T(8,128)(2,1)S(1)}, bf16[256,256]{1,0:T(8,128)(2,1)}, u32[]{:S(2)}) %copy-start.5) | copy-done | bytes 131096
  15.8 0.8 %copy-done.6 = bf16[128,128]{1,0:T(8,128)(2,1)S(1)} copy-done((bf16[128,128]{1,0:T(8,128)(2,1)S(1)}, bf16[128,128]{1,0:T(8,128)(2,1)}, u32[]{:S(2)}) %copy-start.6) | copy-done | bytes 32792
  16.5 0.8 %copy-done.7 = bf16[128,128]{1,0:T(8,128)(2,1)S(1)} copy-done((bf16[128,128]{1,0:T(8,128)(2,1)S(1)}, bf16[128,128]{1,0:T(8,128)(2,1)}, u32[]{:S(2)}) %copy-start.7) | copy-done | bytes 32792
  17.3 0.8 %copy-done.8 = bf16[128,128]{1,0:T(8,128)(2,1)S(1)} copy-done((bf16[128,128]{1,0:T(8,128)(2,1)S(1)}, bf16[128,128]{1,0:T(8,128)(2,1)}, u32[]{:S(2)}) %copy-start.8) | copy-done | bytes 32792
  18.0 0.8 %copy-done.9 = bf16[128,128]{1,0:T(8,128)(2,1)S(1)} copy-done((bf16[128,128]{1,0:T(8,128)(2,1)S(1)}, bf16[128,128]{1,0:T(8,128)(2,1)}, u32[]{:S(2)}) %copy-start.9) | copy-done | bytes 32792
  18.8 1.2 %shard_map.100 = (bf16[2048,128]{1,0:T(8,128)(2,1)S(1)}, bf16[256,256]{1,0:T(8,128)(2,1)S(1)}, bf16[256,256]{1,0:T(8,128)(2,1)S(1)}, bf16[128,128]{1,0:T(8,128)(...) custom-call(bf16[2048,128]{1,0:T(8,128)(2,1)S(1)} %bitcast.4, ...), custom_call_target="tpu_custom_call" | custom-call | bytes 8388608 | tf_op jit(solution)/shard_map/pallas_call | solution.py:227
  20.0 1.0 %collective-permute-done.1.refs_2_ = bf16[2048,128]{1,0:T(8,128)(2,1)S(1)} collective-permute-done((bf16[2048,128]{1,0:T(8,128)(2,1)}, bf16[2048,128]{1,0:T(8,128)(2,1)S(1)}, u32[]{:S(2)}, u32[]{:S(2)}) %collective-permute-start.1) | collective-permute-done | bytes 524320 | tf_op jit(solution)/shard_map/ppermute | solution.py:265
  21.1 0.0 collective-permute-done.refs_1_
  21.1 3.4 %shard_map.101 = (f32[1024,128]{1,0:T(8,128)S(1)}, bf16[1024,128]{1,0:T(8,128)(2,1)S(1)}, bf16[1024,128]{1,0:T(8,128)(2,1)S(1)}, f32[8384,128]{1,0:T(8,128)S(1)}) custom-call(bf16[2048,128]{1,0:T(8,128)(2,1)S(1)} %get-tuple-element.22.refs_0_, bf16[2048,128]{1,0:T(8,128)(2,1)S(1)} %collective-permute-done.refs_1_, ...), custom_call_target="tpu_custom_call" | custom-call | flops 4294967296 | bytes 8388608 | tf_op jit(solution)/shard_map/pallas_call | solution.py:239
  24.5 0.1 collective-permute-start.2
  24.6 5.1 %collective-permute-start.3 = (bf16[1024,128]{1,0:T(8,128)(2,1)S(1)}, bf16[1024,128]{1,0:T(8,128)(2,1)S(1)}, u32[]{:S(2)}, u32[]{:S(2)}) collective-permute-start(bf16[1024,128]{1,0:T(8,128)(2,1)S(1)} %get-tuple-element.34), channel_id=1, source_target_pairs={{0,63},{1,0},{2,1},{3,2},{4,3},{5,4},{6,5},{7,6},{8,7},{9,8},{10,9... | collective-permute-start | bytes 786440 | tf_op jit(solution)/shard_map/ppermute | solution.py:265
  29.8 0.7 %shard_map.102 = (f32[1024,128]{1,0:T(8,128)S(1)}, bf16[1024,128]{1,0:T(8,128)(2,1)S(1)}, bf16[1024,128]{1,0:T(8,128)(2,1)S(1)}) custom-call(bf16[2048,128]{1,0:T(8,128)(2,1)S(1)} %get-tuple-element.22.refs_0_, bf16[2048,128]{1,0:T(8,128)(2,1)S(1)} %collective-permute-done.refs_1_, bf16[2048,128]{1,0:T(8,128)(2,1)S(1)} %collective-permute-done.1.refs_2_, ...), custom_call_target="tpu_custom_call" | custom-call | flops 1073741824 | bytes 8388608 | tf_op jit(solution)/shard_map/pallas_call | solution.py:239
  30.5 0.1 collective-permute-start.4
  30.6 1.8 %collective-permute-start.5 = (bf16[1024,128]{1,0:T(8,128)(2,1)S(1)}, bf16[1024,128]{1,0:T(8,128)(2,1)S(1)}, u32[]{:S(2)}, u32[]{:S(2)}) collective-permute-start(bf16[1024,128]{1,0:T(8,128)(2,1)S(1)} %get-tuple-element.38), channel_id=1, source_target_pairs={{0,63},{1,0},{2,1},{3,2},{4,3},{5,4},{6,5},{7,6},{8,7},{9,8},{10,9... | collective-permute-start | bytes 786440 | tf_op jit(solution)/shard_map/ppermute | solution.py:265
  32.4 3.2 %collective-permute-done.2.refs_1_ = bf16[1024,128]{1,0:T(8,128)(2,1)S(1)} collective-permute-done((bf16[1024,128]{1,0:T(8,128)(2,1)S(1)}, bf16[1024,128]{1,0:T(8,128)(2,1)S(1)}, u32[]{:S(2)}, u32[]{:S(2)}) %collective-permute-start.2) | collective-permute-done | bytes 262176 | tf_op jit(solution)/shard_map/ppermute | solution.py:265
  35.6 0.9 %collective-permute-done.3.refs_2_ = bf16[1024,128]{1,0:T(8,128)(2,1)S(1)} collective-permute-done((bf16[1024,128]{1,0:T(8,128)(2,1)S(1)}, bf16[1024,128]{1,0:T(8,128)(2,1)S(1)}, u32[]{:S(2)}, u32[]{:S(2)}) %collective-permute-start.3) | collective-permute-done | bytes 262176 | tf_op jit(solution)/shard_map/ppermute | solution.py:265
  36.5 4.5 %collective-permute-done.4.refs_4_ = bf16[1024,128]{1,0:T(8,128)(2,1)S(1)} collective-permute-done((bf16[1024,128]{1,0:T(8,128)(2,1)S(1)}, bf16[1024,128]{1,0:T(8,128)(2,1)S(1)}, u32[]{:S(2)}, u32[]{:S(2)}) %collective-permute-start.4) | collective-permute-done | bytes 262176 | tf_op jit(solution)/shard_map/ppermute | solution.py:265
  41.0 0.0 collective-permute-done.5.refs_5_
  41.0 1.0 %shard_map.103 = f32[2048,128]{1,0:T(8,128)} custom-call(f32[1024,128]{1,0:T(8,128)S(1)} %get-tuple-element.32.refs_0_, bf16[1024,128]{1,0:T(8,128)(2,1)S(1)} %collective-permute-done.2.refs_1_, bf16[1024,128]{1,0:T(8,128)(2,1)S(1)} %collective-permute-done.3.refs_2_, f32[1024,128]{1,0:T(8,128)S(1)} %get-tuple-element.36.refs_3_, ...), custom_call_target="tpu_custom_call" | custom-call | flops 1048576 | bytes 3145728 | tf_op jit(solution)/shard_map/pallas_call | solution.py:252
  (4 shorter events, 0.0 us)
Async XLA Ops:
  0.0 21.1 %collective-permute-start.1 = (bf16[2048,128]{1,0:T(8,128)(2,1)}, bf16[2048,128]{1,0:T(8,128)(2,1)S(1)}, u32[]{:S(2)}, u32[]{:S(2)}) collective-permute-start(bf16[2048,128]{1,0:T(8,128)(2,1)} %bitcast.2), channel_id=1, source_target_pairs={{0,1},{1,2},{2,3},{3,4},{4,5},{5,6},{6,7},{7,8},{8,9},{9,10},{10,1... | collective-permute-start | bytes 1572872 | tf_op jit(solution)/shard_map/ppermute | solution.py:265
  1.2 19.9 %collective-permute-start = (bf16[2048,128]{1,0:T(8,128)(2,1)}, bf16[2048,128]{1,0:T(8,128)(2,1)S(1)}, u32[]{:S(2)}, u32[]{:S(2)}) collective-permute-start(bf16[2048,128]{1,0:T(8,128)(2,1)} %bitcast.3), channel_id=1, source_target_pairs={{0,62},{1,63},{2,0},{3,1},{4,2},{5,3},{6,4},{7,5},{8,6},{9,7},{10,... | collective-permute-start | bytes 1572872 | tf_op jit(solution)/shard_map/ppermute | solution.py:265
  9.5 1.6 %copy-start = (f32[4096,128]{1,0:T(8,128)S(1)}, f32[4096,128]{1,0:T(8,128)}, u32[]{:S(2)}) copy-start(f32[4096,128]{1,0:T(8,128)} %constant.22.clone.refs_5_) | copy-start | bytes 6291460
  11.1 1.0 %copy-start.1 = (bf16[1,2048,128]{2,1,0:T(8,128)(2,1)S(1)}, bf16[1,2048,128]{2,1,0:T(8,128)(2,1)}, u32[]{:S(2)}) copy-start(bf16[1,2048,128]{2,1,0:T(8,128)(2,1)} %param.10) | copy-start | bytes 1572868
  12.1 0.9 %copy-start.2 = (bf16[256,256]{1,0:T(8,128)(2,1)S(1)}, bf16[256,256]{1,0:T(8,128)(2,1)}, u32[]{:S(2)}) copy-start(bf16[256,256]{1,0:T(8,128)(2,1)} %constant.26.clone.refs_9_) | copy-start | bytes 393220
  13.0 0.9 %copy-start.3 = (bf16[256,256]{1,0:T(8,128)(2,1)S(1)}, bf16[256,256]{1,0:T(8,128)(2,1)}, u32[]{:S(2)}) copy-start(bf16[256,256]{1,0:T(8,128)(2,1)} %constant.25.clone.refs_8_) | copy-start | bytes 393220
  13.9 0.9 %copy-start.4 = (bf16[256,256]{1,0:T(8,128)(2,1)S(1)}, bf16[256,256]{1,0:T(8,128)(2,1)}, u32[]{:S(2)}) copy-start(bf16[256,256]{1,0:T(8,128)(2,1)} %constant.19.clone.refs_2_) | copy-start | bytes 393220
  14.9 0.9 %copy-start.5 = (bf16[256,256]{1,0:T(8,128)(2,1)S(1)}, bf16[256,256]{1,0:T(8,128)(2,1)}, u32[]{:S(2)}) copy-start(bf16[256,256]{1,0:T(8,128)(2,1)} %constant.18.clone.refs_1_) | copy-start | bytes 393220
  15.8 0.8 %copy-start.6 = (bf16[128,128]{1,0:T(8,128)(2,1)S(1)}, bf16[128,128]{1,0:T(8,128)(2,1)}, u32[]{:S(2)}) copy-start(bf16[128,128]{1,0:T(8,128)(2,1)} %constant.24.clone.refs_7_) | copy-start | bytes 98308
  16.5 0.8 %copy-start.7 = (bf16[128,128]{1,0:T(8,128)(2,1)S(1)}, bf16[128,128]{1,0:T(8,128)(2,1)}, u32[]{:S(2)}) copy-start(bf16[128,128]{1,0:T(8,128)(2,1)} %constant.23.clone.refs_6_) | copy-start | bytes 98308
  17.3 0.8 %copy-start.8 = (bf16[128,128]{1,0:T(8,128)(2,1)S(1)}, bf16[128,128]{1,0:T(8,128)(2,1)}, u32[]{:S(2)}) copy-start(bf16[128,128]{1,0:T(8,128)(2,1)} %constant.21.clone.refs_4_) | copy-start | bytes 98308
  18.0 0.8 %copy-start.9 = (bf16[128,128]{1,0:T(8,128)(2,1)S(1)}, bf16[128,128]{1,0:T(8,128)(2,1)}, u32[]{:S(2)}) copy-start(bf16[128,128]{1,0:T(8,128)(2,1)} %constant.20.clone.refs_3_) | copy-start | bytes 98308
  24.5 11.1 %collective-permute-start.2 = (bf16[1024,128]{1,0:T(8,128)(2,1)S(1)}, bf16[1024,128]{1,0:T(8,128)(2,1)S(1)}, u32[]{:S(2)}, u32[]{:S(2)}) collective-permute-start(bf16[1024,128]{1,0:T(8,128)(2,1)S(1)} %get-tuple-element.33), channel_id=1, source_target_pairs={{0,2},{1,3},{2,4},{3,5},{4,6},{5,7},{6,8},{7,9},{8,10},{9,11},{10,... | collective-permute-start | bytes 786440 | tf_op jit(solution)/shard_map/ppermute | solution.py:265
  24.6 11.9 %collective-permute-start.3 = (bf16[1024,128]{1,0:T(8,128)(2,1)S(1)}, bf16[1024,128]{1,0:T(8,128)(2,1)S(1)}, u32[]{:S(2)}, u32[]{:S(2)}) collective-permute-start(bf16[1024,128]{1,0:T(8,128)(2,1)S(1)} %get-tuple-element.34), channel_id=1, source_target_pairs={{0,63},{1,0},{2,1},{3,2},{4,3},{5,4},{6,5},{7,6},{8,7},{9,8},{10,9... | collective-permute-start | bytes 786440 | tf_op jit(solution)/shard_map/ppermute | solution.py:265
  30.5 10.6 %collective-permute-start.4 = (bf16[1024,128]{1,0:T(8,128)(2,1)S(1)}, bf16[1024,128]{1,0:T(8,128)(2,1)S(1)}, u32[]{:S(2)}, u32[]{:S(2)}) collective-permute-start(bf16[1024,128]{1,0:T(8,128)(2,1)S(1)} %get-tuple-element.37), channel_id=1, source_target_pairs={{0,2},{1,3},{2,4},{3,5},{4,6},{5,7},{6,8},{7,9},{8,10},{9,11},{10,... | collective-permute-start | bytes 786440 | tf_op jit(solution)/shard_map/ppermute | solution.py:265
  30.6 10.5 %collective-permute-start.5 = (bf16[1024,128]{1,0:T(8,128)(2,1)S(1)}, bf16[1024,128]{1,0:T(8,128)(2,1)S(1)}, u32[]{:S(2)}, u32[]{:S(2)}) collective-permute-start(bf16[1024,128]{1,0:T(8,128)(2,1)S(1)} %get-tuple-element.38), channel_id=1, source_target_pairs={{0,63},{1,0},{2,1},{3,2},{4,3},{5,4},{6,5},{7,6},{8,7},{9,8},{10,9... | collective-permute-start | bytes 786440 | tf_op jit(solution)/shard_map/ppermute | solution.py:265

commit v6 on v5

--- a/solution.py
+++ b/solution.py
@@ -17,6 +17,7 @@
 PITCH = 129
 ROWS = 64 * PITCH + LANES
 PARTS = 2
+CHUNKS = 2
 MIXING = 0.25
 
 
@@ -197,18 +198,16 @@
     last_stages(part, PARTS, *orbitals, y_inv, back_low, back_high, spec, outputs, flat)
 
 
-def finish_kernel(*refs):
-    groups, out_ref, held, sem = refs[:-3], refs[-3], refs[-2], refs[-1]
-    rows = groups[0].shape[0]
+def finish_kernel(part, total, one, two, *refs):
+    out_ref, held, sem = refs[-3:]
+    rows = total.shape[0] // CHUNKS
     copies = []
-    for n in range(len(groups) // 3):
-        total, one, two = groups[3 * n : 3 * n + 3]
-        for half in range(2):
-            here = pl.ds(half * (rows // 2), rows // 2)
-            there = pl.ds(n * rows + half * (rows // 2), rows // 2)
-            held[there, :] = total[here, :] + one[here, :].astype(jnp.float32) + two[here, :].astype(jnp.float32)
-            copies.append(pltpu.make_async_copy(held.at[there], out_ref.at[there], sem.at[2 * n + half]))
-            copies[-1].start()
+    for n in range(CHUNKS):
+        here = pl.ds(n * rows, rows)
+        there = pl.ds((part * CHUNKS + n) * rows, rows)
+        held[here, :] = total[here, :] + one[here, :].astype(jnp.float32) + two[here, :].astype(jnp.float32)
+        copies.append(pltpu.make_async_copy(held.at[here], out_ref.at[there], sem.at[n]))
+        copies[-1].start()
     for copy in copies:
         copy.wait()
 
@@ -247,17 +246,18 @@
     )(*operands)
 
 
-def finished(groups, rows):
-    operands = [x for group in groups for x in group]
+def finished(part, terms, earlier):
+    rows = terms[0].shape[0]
     return pl.pallas_call(
-        finish_kernel,
-        out_shape=jax.ShapeDtypeStruct((rows, LANES), jnp.float32),
-        in_specs=[pl.BlockSpec(memory_space=pltpu.VMEM)] * len(operands),
+        functools.partial(finish_kernel, part),
+        out_shape=jax.ShapeDtypeStruct((PARTS * rows, LANES), jnp.float32),
+        in_specs=[pl.BlockSpec(memory_space=pltpu.VMEM)] * 3 + [pl.BlockSpec(memory_space=pl.ANY)] * len(earlier),
         out_specs=pl.BlockSpec(memory_space=pl.ANY),
-        scratch_shapes=[pltpu.VMEM((rows, LANES), jnp.float32), pltpu.SemaphoreType.DMA((2 * len(groups),))],
+        scratch_shapes=[pltpu.VMEM((rows, LANES), jnp.float32), pltpu.SemaphoreType.DMA((CHUNKS,))],
+        input_output_aliases={3: 0} if earlier else {},
         compiler_params=pltpu.CompilerParams(vmem_limit_bytes=16 * 1024 * 1024),
-        cost_estimate=pl.CostEstimate(flops=2**20, bytes_accessed=3 << 20, transcendentals=0),
-    )(*operands)
+        cost_estimate=pl.CostEstimate(flops=2**20, bytes_accessed=2 << 20, transcendentals=0),
+    )(*terms, *earlier)
 
 
 def shifted(x, by):
@@ -281,7 +281,10 @@
             terms = vmem_call(functools.partial(second_kernel, n), part, scratch[1:], operands, 2**30)
         total, to_ahead, to_behind = terms
         groups.append([total, shifted(to_ahead, 2), shifted(to_behind, -1)])
-    return finished(groups, rows)[None]
+    out = []
+    for n, group in enumerate(groups):
+        out = [finished(n, group, out)]
+    return out[0][None]
 
 
 def solution(mesh):

time: 42.6 us -> 42.4 us (level)
  waiting for transfers between devices: 9.68 us -> 8.83 us
  Pallas kernels: 6.43 us -> 7.08 us
    ppermute x6, waiting for transfers between devices: 9.68 us -> 8.83 us  [shifted(): lax.ppermute(x, 'band', [(i, (i + by) % count) for i in range(count)])]
    pallas_call x1 -> x2, Pallas kernels: 1.03 us -> 1.68 us  [finished(): pl.pallas_call(functools.partial(finish_kernel, part), out_shape=jax.Shap...]
  transfers between devices with their start and end apart: 6 -> 6, of which waited for: 4 -> 4; matrix products, arithmetic and copies ran while one was open for 0% -> 0% of each run, Pallas kernels for 5% -> 7%
where the time goes in v6:
time: 42.4 us; the launch traced here: 41.9 us
  starting transfers between devices  16.6 us (39%)
  local copies, waits for them, and re-layouts  9.28 us (22%)
  waiting for transfers between devices  8.83 us (21%)
  Pallas kernels  7.08 us (17%)
    ppermute x6, starting transfers between devices, shifted(): lax.ppermute(x, 'band', [(i, (i + by) % count) for i in range(count)])  16.6 us
    unnamed x20, local copies, waits for them, and re-layouts  9.28 us
    ppermute x6, waiting for transfers between devices, shifted(): lax.ppermute(x, 'band', [(i, (i + by) % count) for i in range(count)])  8.83 us
    pallas_call x2, Pallas kernels, vmem_call(): pl.pallas_call(kernel, out_shape=outputs, in_specs=[pl.BlockSpec(memory_s...  4.17 us
    pallas_call x2, Pallas kernels, finished(): pl.pallas_call(functools.partial(finish_kernel, part), out_shape=jax.Shap...  1.68 us
    pallas_call x1, Pallas kernels, held_in_vmem(): pl.pallas_call(hold_kernel, out_shape=[pltpu.VMEM(x.shape, x.dtype) for x...  1.23 us
  transfers between devices with their start and end apart: 6, of which 4 were waited for; matrix products, arithmetic and copies ran while one was open for 0% of the time, Pallas kernels for 7%

profile of v6, /device:TPU:4, one launch (start us, length us, event | category | flops | bytes accessed | tf_op | source)
XLA Modules:
  0.0 41.9 jit_solution(2631273926125653702)
XLA Ops:
  0.0 1.2 %collective-permute-start.1 = (bf16[2048,128]{1,0:T(8,128)(2,1)}, bf16[2048,128]{1,0:T(8,128)(2,1)S(1)}, u32[]{:S(2)}, u32[]{:S(2)}) collective-permute-start(bf16[2048,128]{1,0:T(8,128)(2,1)} %bitcast.2), channel_id=1, source_target_pairs={{0,1},{1,2},{2,3},{3,4},{4,5},{5,6},{6,7},{7,8},{8,9},{9,10},{10,1... | collective-permute-start | bytes 1572872 | tf_op jit(solution)/shard_map/ppermute | solution.py:265
  1.2 8.3 %collective-permute-start = (bf16[2048,128]{1,0:T(8,128)(2,1)}, bf16[2048,128]{1,0:T(8,128)(2,1)S(1)}, u32[]{:S(2)}, u32[]{:S(2)}) collective-permute-start(bf16[2048,128]{1,0:T(8,128)(2,1)} %bitcast.3), channel_id=1, source_target_pairs={{0,62},{1,63},{2,0},{3,1},{4,2},{5,3},{6,4},{7,5},{8,6},{9,7},{10,... | collective-permute-start | bytes 1572872 | tf_op jit(solution)/shard_map/ppermute | solution.py:265
  9.5 0.0 copy-start
  9.5 1.6 %copy-done = f32[4096,128]{1,0:T(8,128)S(1)} copy-done((f32[4096,128]{1,0:T(8,128)S(1)}, f32[4096,128]{1,0:T(8,128)}, u32[]{:S(2)}) %copy-start) | copy-done | bytes 2097176
  11.1 0.0 copy-start.1
  11.1 1.0 %copy-done.1 = bf16[1,2048,128]{2,1,0:T(8,128)(2,1)S(1)} copy-done((bf16[1,2048,128]{2,1,0:T(8,128)(2,1)S(1)}, bf16[1,2048,128]{2,1,0:T(8,128)(2,1)}, u32[]{:S(2)}) %copy-start.1) | copy-done | bytes 524312
  12.1 0.0 copy-start.2
  12.1 0.9 %copy-done.2 = bf16[256,256]{1,0:T(8,128)(2,1)S(1)} copy-done((bf16[256,256]{1,0:T(8,128)(2,1)S(1)}, bf16[256,256]{1,0:T(8,128)(2,1)}, u32[]{:S(2)}) %copy-start.2) | copy-done | bytes 131096
  13.0 0.0 copy-start.3
  13.0 0.9 %copy-done.3 = bf16[256,256]{1,0:T(8,128)(2,1)S(1)} copy-done((bf16[256,256]{1,0:T(8,128)(2,1)S(1)}, bf16[256,256]{1,0:T(8,128)(2,1)}, u32[]{:S(2)}) %copy-start.3) | copy-done | bytes 131096
  13.9 0.0 copy-start.4
  14.0 0.9 %copy-done.4 = bf16[256,256]{1,0:T(8,128)(2,1)S(1)} copy-done((bf16[256,256]{1,0:T(8,128)(2,1)S(1)}, bf16[256,256]{1,0:T(8,128)(2,1)}, u32[]{:S(2)}) %copy-start.4) | copy-done | bytes 131096
  14.9 0.9 %copy-done.5 = bf16[256,256]{1,0:T(8,128)(2,1)S(1)} copy-done((bf16[256,256]{1,0:T(8,128)(2,1)S(1)}, bf16[256,256]{1,0:T(8,128)(2,1)}, u32[]{:S(2)}) %copy-start.5) | copy-done | bytes 131096
  15.8 0.8 %copy-done.6 = bf16[128,128]{1,0:T(8,128)(2,1)S(1)} copy-done((bf16[128,128]{1,0:T(8,128)(2,1)S(1)}, bf16[128,128]{1,0:T(8,128)(2,1)}, u32[]{:S(2)}) %copy-start.6) | copy-done | bytes 32792
  16.5 0.8 %copy-done.7 = bf16[128,128]{1,0:T(8,128)(2,1)S(1)} copy-done((bf16[128,128]{1,0:T(8,128)(2,1)S(1)}, bf16[128,128]{1,0:T(8,128)(2,1)}, u32[]{:S(2)}) %copy-start.7) | copy-done | bytes 32792
  17.3 0.8 %copy-done.8 = bf16[128,128]{1,0:T(8,128)(2,1)S(1)} copy-done((bf16[128,128]{1,0:T(8,128)(2,1)S(1)}, bf16[128,128]{1,0:T(8,128)(2,1)}, u32[]{:S(2)}) %copy-start.8) | copy-done | bytes 32792
  18.0 0.8 %copy-done.9 = bf16[128,128]{1,0:T(8,128)(2,1)S(1)} copy-done((bf16[128,128]{1,0:T(8,128)(2,1)S(1)}, bf16[128,128]{1,0:T(8,128)(2,1)}, u32[]{:S(2)}) %copy-start.9) | copy-done | bytes 32792
  18.8 1.2 %shard_map.100 = (bf16[2048,128]{1,0:T(8,128)(2,1)S(1)}, bf16[256,256]{1,0:T(8,128)(2,1)S(1)}, bf16[256,256]{1,0:T(8,128)(2,1)S(1)}, bf16[128,128]{1,0:T(8,128)(...) custom-call(bf16[2048,128]{1,0:T(8,128)(2,1)S(1)} %bitcast.4, ...), custom_call_target="tpu_custom_call" | custom-call | bytes 8388608 | tf_op jit(solution)/shard_map/pallas_call | solution.py:226
  20.0 1.0 %collective-permute-done.1.refs_2_ = bf16[2048,128]{1,0:T(8,128)(2,1)S(1)} collective-permute-done((bf16[2048,128]{1,0:T(8,128)(2,1)}, bf16[2048,128]{1,0:T(8,128)(2,1)S(1)}, u32[]{:S(2)}, u32[]{:S(2)}) %collective-permute-start.1) | collective-permute-done | bytes 524320 | tf_op jit(solution)/shard_map/ppermute | solution.py:265
  21.1 0.0 collective-permute-done.refs_1_
  21.1 3.4 %shard_map.101 = (f32[1024,128]{1,0:T(8,128)S(1)}, bf16[1024,128]{1,0:T(8,128)(2,1)S(1)}, bf16[1024,128]{1,0:T(8,128)(2,1)S(1)}, f32[8384,128]{1,0:T(8,128)S(1)}) custom-call(bf16[2048,128]{1,0:T(8,128)(2,1)S(1)} %get-tuple-element.22.refs_0_, bf16[2048,128]{1,0:T(8,128)(2,1)S(1)} %collective-permute-done.refs_1_, ...), custom_call_target="tpu_custom_call" | custom-call | flops 4294967296 | bytes 8388608 | tf_op jit(solution)/shard_map/pallas_call | solution.py:238
  24.5 0.1 collective-permute-start.4
  24.6 5.1 %collective-permute-start.5 = (bf16[1024,128]{1,0:T(8,128)(2,1)S(1)}, bf16[1024,128]{1,0:T(8,128)(2,1)S(1)}, u32[]{:S(2)}, u32[]{:S(2)}) collective-permute-start(bf16[1024,128]{1,0:T(8,128)(2,1)S(1)} %get-tuple-element.38), channel_id=1, source_target_pairs={{0,63},{1,0},{2,1},{3,2},{4,3},{5,4},{6,5},{7,6},{8,7},{9,8},{10,9... | collective-permute-start | bytes 786440 | tf_op jit(solution)/shard_map/ppermute | solution.py:265
  29.8 0.7 %shard_map.102 = (f32[1024,128]{1,0:T(8,128)S(1)}, bf16[1024,128]{1,0:T(8,128)(2,1)S(1)}, bf16[1024,128]{1,0:T(8,128)(2,1)S(1)}) custom-call(bf16[2048,128]{1,0:T(8,128)(2,1)S(1)} %get-tuple-element.22.refs_0_, bf16[2048,128]{1,0:T(8,128)(2,1)S(1)} %collective-permute-done.refs_1_, bf16[2048,128]{1,0:T(8,128)(2,1)S(1)} %collective-permute-done.1.refs_2_, ...), custom_call_target="tpu_custom_call" | custom-call | flops 1073741824 | bytes 8388608 | tf_op jit(solution)/shard_map/pallas_call | solution.py:238
  30.5 0.1 collective-permute-start.2
  30.6 1.8 %collective-permute-start.3 = (bf16[1024,128]{1,0:T(8,128)(2,1)S(1)}, bf16[1024,128]{1,0:T(8,128)(2,1)S(1)}, u32[]{:S(2)}, u32[]{:S(2)}) collective-permute-start(bf16[1024,128]{1,0:T(8,128)(2,1)S(1)} %get-tuple-element.35), channel_id=1, source_target_pairs={{0,63},{1,0},{2,1},{3,2},{4,3},{5,4},{6,5},{7,6},{8,7},{9,8},{10,9... | collective-permute-start | bytes 786440 | tf_op jit(solution)/shard_map/ppermute | solution.py:265
  32.4 3.2 %collective-permute-done.4.one = bf16[1024,128]{1,0:T(8,128)(2,1)S(1)} collective-permute-done((bf16[1024,128]{1,0:T(8,128)(2,1)S(1)}, bf16[1024,128]{1,0:T(8,128)(2,1)S(1)}, u32[]{:S(2)}, u32[]{:S(2)}) %collective-permute-start.4) | collective-permute-done | bytes 262176 | tf_op jit(solution)/shard_map/ppermute | solution.py:265
  35.6 0.9 %collective-permute-done.5.two = bf16[1024,128]{1,0:T(8,128)(2,1)S(1)} collective-permute-done((bf16[1024,128]{1,0:T(8,128)(2,1)S(1)}, bf16[1024,128]{1,0:T(8,128)(2,1)S(1)}, u32[]{:S(2)}, u32[]{:S(2)}) %collective-permute-start.5) | collective-permute-done | bytes 262176 | tf_op jit(solution)/shard_map/ppermute | solution.py:265
  36.5 0.8 %shard_map.103.refs_0_ = f32[2048,128]{1,0:T(8,128)} custom-call(f32[1024,128]{1,0:T(8,128)S(1)} %get-tuple-element.36.total, bf16[1024,128]{1,0:T(8,128)(2,1)S(1)} %collective-permute-done.4.one, bf16[1024,128]{1,0:T(8,128)(2,1)S(1)} %collective-permute-done.5.two), custom_call_target="tpu_custom_call" | custom-call | flops 1048576 | bytes 2097152 | tf_op jit(solution)/shard_map/pallas_call | solution.py:251
  37.4 3.7 %collective-permute-done.2.one = bf16[1024,128]{1,0:T(8,128)(2,1)S(1)} collective-permute-done((bf16[1024,128]{1,0:T(8,128)(2,1)S(1)}, bf16[1024,128]{1,0:T(8,128)(2,1)S(1)}, u32[]{:S(2)}, u32[]{:S(2)}) %collective-permute-start.2) | collective-permute-done | bytes 262176 | tf_op jit(solution)/shard_map/ppermute | solution.py:265
  41.0 0.0 collective-permute-done.3.two
  41.0 0.8 %shard_map.104 = f32[2048,128]{1,0:T(8,128)} custom-call(f32[1024,128]{1,0:T(8,128)S(1)} %get-tuple-element.33.total, bf16[1024,128]{1,0:T(8,128)(2,1)S(1)} %collective-permute-done.2.one, bf16[1024,128]{1,0:T(8,128)(2,1)S(1)} %collective-permute-done.3.two, f32[2048,128]{1,0:T(8,128)} %shard_map.103.refs_0_), custom_call_target="tpu_custom_call", output_to_operand_aliasing={{}: (3, {})} | custom-call | flops 1048576 | bytes 2097152 | tf_op jit(solution)/shard_map/pallas_call | solution.py:251
  (5 shorter events, 0.0 us)
Async XLA Ops:
  0.0 21.1 %collective-permute-start.1 = (bf16[2048,128]{1,0:T(8,128)(2,1)}, bf16[2048,128]{1,0:T(8,128)(2,1)S(1)}, u32[]{:S(2)}, u32[]{:S(2)}) collective-permute-start(bf16[2048,128]{1,0:T(8,128)(2,1)} %bitcast.2), channel_id=1, source_target_pairs={{0,1},{1,2},{2,3},{3,4},{4,5},{5,6},{6,7},{7,8},{8,9},{9,10},{10,1... | collective-permute-start | bytes 1572872 | tf_op jit(solution)/shard_map/ppermute | solution.py:265
  1.2 19.9 %collective-permute-start = (bf16[2048,128]{1,0:T(8,128)(2,1)}, bf16[2048,128]{1,0:T(8,128)(2,1)S(1)}, u32[]{:S(2)}, u32[]{:S(2)}) collective-permute-start(bf16[2048,128]{1,0:T(8,128)(2,1)} %bitcast.3), channel_id=1, source_target_pairs={{0,62},{1,63},{2,0},{3,1},{4,2},{5,3},{6,4},{7,5},{8,6},{9,7},{10,... | collective-permute-start | bytes 1572872 | tf_op jit(solution)/shard_map/ppermute | solution.py:265
  9.5 1.6 %copy-start = (f32[4096,128]{1,0:T(8,128)S(1)}, f32[4096,128]{1,0:T(8,128)}, u32[]{:S(2)}) copy-start(f32[4096,128]{1,0:T(8,128)} %constant.22.clone.refs_5_) | copy-start | bytes 6291460
  11.1 1.0 %copy-start.1 = (bf16[1,2048,128]{2,1,0:T(8,128)(2,1)S(1)}, bf16[1,2048,128]{2,1,0:T(8,128)(2,1)}, u32[]{:S(2)}) copy-start(bf16[1,2048,128]{2,1,0:T(8,128)(2,1)} %param.10) | copy-start | bytes 1572868
  12.1 0.9 %copy-start.2 = (bf16[256,256]{1,0:T(8,128)(2,1)S(1)}, bf16[256,256]{1,0:T(8,128)(2,1)}, u32[]{:S(2)}) copy-start(bf16[256,256]{1,0:T(8,128)(2,1)} %constant.26.clone.refs_9_) | copy-start | bytes 393220
  13.0 0.9 %copy-start.3 = (bf16[256,256]{1,0:T(8,128)(2,1)S(1)}, bf16[256,256]{1,0:T(8,128)(2,1)}, u32[]{:S(2)}) copy-start(bf16[256,256]{1,0:T(8,128)(2,1)} %constant.25.clone.refs_8_) | copy-start | bytes 393220
  13.9 0.9 %copy-start.4 = (bf16[256,256]{1,0:T(8,128)(2,1)S(1)}, bf16[256,256]{1,0:T(8,128)(2,1)}, u32[]{:S(2)}) copy-start(bf16[256,256]{1,0:T(8,128)(2,1)} %constant.19.clone.refs_2_) | copy-start | bytes 393220
  14.9 0.9 %copy-start.5 = (bf16[256,256]{1,0:T(8,128)(2,1)S(1)}, bf16[256,256]{1,0:T(8,128)(2,1)}, u32[]{:S(2)}) copy-start(bf16[256,256]{1,0:T(8,128)(2,1)} %constant.18.clone.refs_1_) | copy-start | bytes 393220
  15.8 0.8 %copy-start.6 = (bf16[128,128]{1,0:T(8,128)(2,1)S(1)}, bf16[128,128]{1,0:T(8,128)(2,1)}, u32[]{:S(2)}) copy-start(bf16[128,128]{1,0:T(8,128)(2,1)} %constant.24.clone.refs_7_) | copy-start | bytes 98308
  16.5 0.8 %copy-start.7 = (bf16[128,128]{1,0:T(8,128)(2,1)S(1)}, bf16[128,128]{1,0:T(8,128)(2,1)}, u32[]{:S(2)}) copy-start(bf16[128,128]{1,0:T(8,128)(2,1)} %constant.23.clone.refs_6_) | copy-start | bytes 98308
  17.3 0.8 %copy-start.8 = (bf16[128,128]{1,0:T(8,128)(2,1)S(1)}, bf16[128,128]{1,0:T(8,128)(2,1)}, u32[]{:S(2)}) copy-start(bf16[128,128]{1,0:T(8,128)(2,1)} %constant.21.clone.refs_4_) | copy-start | bytes 98308
  18.0 0.8 %copy-start.9 = (bf16[128,128]{1,0:T(8,128)(2,1)S(1)}, bf16[128,128]{1,0:T(8,128)(2,1)}, u32[]{:S(2)}) copy-start(bf16[128,128]{1,0:T(8,128)(2,1)} %constant.20.clone.refs_3_) | copy-start | bytes 98308
  24.5 11.1 %collective-permute-start.4 = (bf16[1024,128]{1,0:T(8,128)(2,1)S(1)}, bf16[1024,128]{1,0:T(8,128)(2,1)S(1)}, u32[]{:S(2)}, u32[]{:S(2)}) collective-permute-start(bf16[1024,128]{1,0:T(8,128)(2,1)S(1)} %get-tuple-element.37), channel_id=1, source_target_pairs={{0,2},{1,3},{2,4},{3,5},{4,6},{5,7},{6,8},{7,9},{8,10},{9,11},{10,... | collective-permute-start | bytes 786440 | tf_op jit(solution)/shard_map/ppermute | solution.py:265
  24.6 11.9 %collective-permute-start.5 = (bf16[1024,128]{1,0:T(8,128)(2,1)S(1)}, bf16[1024,128]{1,0:T(8,128)(2,1)S(1)}, u32[]{:S(2)}, u32[]{:S(2)}) collective-permute-start(bf16[1024,128]{1,0:T(8,128)(2,1)S(1)} %get-tuple-element.38), channel_id=1, source_target_pairs={{0,63},{1,0},{2,1},{3,2},{4,3},{5,4},{6,5},{7,6},{8,7},{9,8},{10,9... | collective-permute-start | bytes 786440 | tf_op jit(solution)/shard_map/ppermute | solution.py:265
  30.5 10.6 %collective-permute-start.2 = (bf16[1024,128]{1,0:T(8,128)(2,1)S(1)}, bf16[1024,128]{1,0:T(8,128)(2,1)S(1)}, u32[]{:S(2)}, u32[]{:S(2)}) collective-permute-start(bf16[1024,128]{1,0:T(8,128)(2,1)S(1)} %get-tuple-element.34), channel_id=1, source_target_pairs={{0,2},{1,3},{2,4},{3,5},{4,6},{5,7},{6,8},{7,9},{8,10},{9,11},{10,... | collective-permute-start | bytes 786440 | tf_op jit(solution)/shard_map/ppermute | solution.py:265
  30.6 10.5 %collective-permute-start.3 = (bf16[1024,128]{1,0:T(8,128)(2,1)S(1)}, bf16[1024,128]{1,0:T(8,128)(2,1)S(1)}, u32[]{:S(2)}, u32[]{:S(2)}) collective-permute-start(bf16[1024,128]{1,0:T(8,128)(2,1)S(1)} %get-tuple-element.35), channel_id=1, source_target_pairs={{0,63},{1,0},{2,1},{3,2},{4,3},{5,4},{6,5},{7,6},{8,7},{9,8},{10,9... | collective-permute-start | bytes 786440 | tf_op jit(solution)/shard_map/ppermute | solution.py:265

commit v7 on v6

--- a/solution.py
+++ b/solution.py
@@ -185,7 +185,9 @@
 
 def first_kernel(*refs):
     orbitals, refs = refs[:3], refs[3:]
-    into_low, into_high, y_fwd, x_fwd, kernel, x_inv, y_inv, back_low, back_high, *refs = refs
+    wide_tables, narrow_tables, kernel, *refs = refs
+    into_low, into_high, back_low, back_high = (wide_tables.at[n] for n in range(4))
+    y_fwd, x_fwd, x_inv, y_inv = (narrow_tables.at[n] for n in range(4))
     *outputs, spec, planes, flat = refs
     forward_stages(*orbitals, into_low, into_high, y_fwd, x_fwd, kernel, x_inv, planes, spec, flat)
     last_stages(0, PARTS, *orbitals, y_inv, back_low, back_high, spec, outputs, flat)
@@ -193,7 +195,8 @@
 
 def second_kernel(part, *refs):
     orbitals, refs = refs[:3], refs[3:]
-    y_inv, back_low, back_high, spec, *refs = refs
+    wide_tables, narrow_tables, spec, *refs = refs
+    y_inv, back_low, back_high = narrow_tables.at[3], wide_tables.at[2], wide_tables.at[3]
     *outputs, flat = refs
     last_stages(part, PARTS, *orbitals, y_inv, back_low, back_high, spec, outputs, flat)
 
@@ -269,7 +272,9 @@
     rows = orbitals.shape[1]
     behind = shifted(orbitals[0], 1)
     ahead = shifted(orbitals[0], -2)
-    own, *tables = held_in_vmem([orbitals[0], *(jnp.asarray(t) for t in make_tables())])
+    t = make_tables()
+    packed = np.stack([t[0], t[1], t[7], t[8]]), np.stack([t[2], t[3], t[5], t[6]]), t[4]
+    own, *tables = held_in_vmem([orbitals[0], *(jnp.asarray(x) for x in packed)])
     part = [pltpu.VMEM((rows // PARTS, LANES), t) for t in (jnp.float32, jnp.bfloat16, jnp.bfloat16)]
     planes = pltpu.VMEM((ROWS, LANES), jnp.float32)
     scratch = [planes, pltpu.VMEM((rows, SLOTS * LANES), jnp.bfloat16)]
@@ -277,7 +282,7 @@
     groups = []
     for n in range(PARTS):
         if n > 0:
-            operands = [own, ahead, behind, *tables[-3:], spec]
+            operands = [own, ahead, behind, *tables[:2], spec]
             terms = vmem_call(functools.partial(second_kernel, n), part, scratch[1:], operands, 2**30)
         total, to_ahead, to_behind = terms
         groups.append([total, shifted(to_ahead, 2), shifted(to_behind, -1)])

time: 42.4 us -> 42.1 us (level)
  waiting for transfers between devices: 8.83 us -> 14.4 us
  local copies, waits for them, and re-layouts: 9.28 us -> 4.58 us
  Pallas kernels: 7.08 us -> 6.27 us
    ppermute x6, waiting for transfers between devices: 8.83 us -> 14.4 us  [shifted(): lax.ppermute(x, 'band', [(i, (i + by) % count) for i in range(count)])]
    unnamed x20 -> x8, local copies, waits for them, and re-layouts: 9.28 us -> 4.58 us
    pallas_call x1, Pallas kernels: 1.23 us -> 0.42 us  [held_in_vmem(): pl.pallas_call(hold_kernel, out_shape=[pltpu.VMEM(x.shape, x.dtype) for x...]
  transfers between devices with their start and end apart: 6 -> 6, of which waited for: 4 -> 4; matrix products, arithmetic and copies ran while one was open for 0% -> 0% of each run, Pallas kernels for 7% -> 5%
where the time goes in v7:
time: 42.1 us; the launch traced here: 41.9 us
  starting transfers between devices  16.6 us (39%)
  waiting for transfers between devices  14.4 us (34%)
  Pallas kernels  6.27 us (15%)
  local copies, waits for them, and re-layouts  4.58 us (11%)
    ppermute x6, starting transfers between devices, shifted(): lax.ppermute(x, 'band', [(i, (i + by) % count) for i in range(count)])  16.6 us
    ppermute x6, waiting for transfers between devices, shifted(): lax.ppermute(x, 'band', [(i, (i + by) % count) for i in range(count)])  14.4 us
    unnamed x8, local copies, waits for them, and re-layouts  4.58 us
    pallas_call x2, Pallas kernels, vmem_call(): pl.pallas_call(kernel, out_shape=outputs, in_specs=[pl.BlockSpec(memory_s...  4.17 us
    pallas_call x2, Pallas kernels, finished(): pl.pallas_call(functools.partial(finish_kernel, part), out_shape=jax.Shap...  1.68 us
  transfers between devices with their start and end apart: 6, of which 4 were waited for; matrix products, arithmetic and copies ran while one was open for 0% of the time, Pallas kernels for 5%

profile of v7, /device:TPU:4, one launch (start us, length us, event | category | flops | bytes accessed | tf_op | source)
XLA Modules:
  0.0 41.9 jit_solution(936762423211263209)
XLA Ops:
  0.0 1.2 %collective-permute-start.1 = (bf16[2048,128]{1,0:T(8,128)(2,1)}, bf16[2048,128]{1,0:T(8,128)(2,1)S(1)}, u32[]{:S(2)}, u32[]{:S(2)}) collective-permute-start(bf16[2048,128]{1,0:T(8,128)(2,1)} %bitcast.2), channel_id=1, source_target_pairs={{0,1},{1,2},{2,3},{3,4},{4,5},{5,6},{6,7},{7,8},{8,9},{9,10},{10,1... | collective-permute-start | bytes 1572872 | tf_op jit(solution)/shard_map/ppermute | solution.py:268
  1.2 8.3 %collective-permute-start = (bf16[2048,128]{1,0:T(8,128)(2,1)}, bf16[2048,128]{1,0:T(8,128)(2,1)S(1)}, u32[]{:S(2)}, u32[]{:S(2)}) collective-permute-start(bf16[2048,128]{1,0:T(8,128)(2,1)} %bitcast.3), channel_id=1, source_target_pairs={{0,62},{1,63},{2,0},{3,1},{4,2},{5,3},{6,4},{7,5},{8,6},{9,7},{10,... | collective-permute-start | bytes 1572872 | tf_op jit(solution)/shard_map/ppermute | solution.py:268
  9.5 0.0 copy-start
  9.5 1.6 %copy-done = f32[4096,128]{1,0:T(8,128)S(1)} copy-done((f32[4096,128]{1,0:T(8,128)S(1)}, f32[4096,128]{1,0:T(8,128)}, u32[]{:S(2)}) %copy-start) | copy-done | bytes 2097176
  11.1 0.0 copy-start.1
  11.1 1.0 %copy-done.1 = bf16[1,2048,128]{2,1,0:T(8,128)(2,1)S(1)} copy-done((bf16[1,2048,128]{2,1,0:T(8,128)(2,1)S(1)}, bf16[1,2048,128]{2,1,0:T(8,128)(2,1)}, u32[]{:S(2)}) %copy-start.1) | copy-done | bytes 524312
  12.1 0.0 copy-start.2
  12.1 1.0 %copy-done.2 = bf16[4,256,256]{2,1,0:T(8,128)(2,1)S(1)} copy-done((bf16[4,256,256]{2,1,0:T(8,128)(2,1)S(1)}, bf16[4,256,256]{2,1,0:T(8,128)(2,1)}, u32[]{:S(2)}) %copy-start.2) | copy-done | bytes 524312
  13.2 0.0 copy-start.3
  13.2 0.9 %copy-done.3 = bf16[4,128,128]{2,1,0:T(8,128)(2,1)S(1)} copy-done((bf16[4,128,128]{2,1,0:T(8,128)(2,1)S(1)}, bf16[4,128,128]{2,1,0:T(8,128)(2,1)}, u32[]{:S(2)}) %copy-start.3) | copy-done | bytes 131096
  14.1 0.4 shard_map.46
  14.5 6.6 %collective-permute-done.1.refs_2_ = bf16[2048,128]{1,0:T(8,128)(2,1)S(1)} collective-permute-done((bf16[2048,128]{1,0:T(8,128)(2,1)}, bf16[2048,128]{1,0:T(8,128)(2,1)S(1)}, u32[]{:S(2)}, u32[]{:S(2)}) %collective-permute-start.1) | collective-permute-done | bytes 524320 | tf_op jit(solution)/shard_map/ppermute | solution.py:268
  21.1 0.0 collective-permute-done.refs_1_
  21.1 3.4 %shard_map.47 = (f32[1024,128]{1,0:T(8,128)S(1)}, bf16[1024,128]{1,0:T(8,128)(2,1)S(1)}, bf16[1024,128]{1,0:T(8,128)(2,1)S(1)}, f32[8384,128]{1,0:T(8,128)S(1)}) custom-call(bf16[2048,128]{1,0:T(8,128)(2,1)S(1)} %get-tuple-element.16.refs_0_, bf16[2048,128]{1,0:T(8,128)(2,1)S(1)} %collective-permute-done.refs_1_, ...), custom_call_target="tpu_custom_call" | custom-call | flops 4294967296 | bytes 8388608 | tf_op jit(solution)/shard_map/pallas_call | solution.py:241
  24.5 0.1 collective-permute-start.4
  24.6 5.1 %collective-permute-start.5 = (bf16[1024,128]{1,0:T(8,128)(2,1)S(1)}, bf16[1024,128]{1,0:T(8,128)(2,1)S(1)}, u32[]{:S(2)}, u32[]{:S(2)}) collective-permute-start(bf16[1024,128]{1,0:T(8,128)(2,1)S(1)} %get-tuple-element.26), channel_id=1, source_target_pairs={{0,63},{1,0},{2,1},{3,2},{4,3},{5,4},{6,5},{7,6},{8,7},{9,8},{10,9... | collective-permute-start | bytes 786440 | tf_op jit(solution)/shard_map/ppermute | solution.py:268
  29.8 0.7 %shard_map.48 = (f32[1024,128]{1,0:T(8,128)S(1)}, bf16[1024,128]{1,0:T(8,128)(2,1)S(1)}, bf16[1024,128]{1,0:T(8,128)(2,1)S(1)}) custom-call(bf16[2048,128]{1,0:T(8,128)(2,1)S(1)} %get-tuple-element.16.refs_0_, bf16[2048,128]{1,0:T(8,128)(2,1)S(1)} %collective-permute-done.refs_1_, bf16[2048,128]{1,0:T(8,128)(2,1)S(1)} %collective-permute-done.1.refs_2_, ...), custom_call_target="tpu_custom_call" | custom-call | flops 1073741824 | bytes 8388608 | tf_op jit(solution)/shard_map/pallas_call | solution.py:241
  30.5 0.1 collective-permute-start.2
  30.6 1.8 %collective-permute-start.3 = (bf16[1024,128]{1,0:T(8,128)(2,1)S(1)}, bf16[1024,128]{1,0:T(8,128)(2,1)S(1)}, u32[]{:S(2)}, u32[]{:S(2)}) collective-permute-start(bf16[1024,128]{1,0:T(8,128)(2,1)S(1)} %get-tuple-element.23), channel_id=1, source_target_pairs={{0,63},{1,0},{2,1},{3,2},{4,3},{5,4},{6,5},{7,6},{8,7},{9,8},{10,9... | collective-permute-start | bytes 786440 | tf_op jit(solution)/shard_map/ppermute | solution.py:268
  32.4 3.2 %collective-permute-done.4.one = bf16[1024,128]{1,0:T(8,128)(2,1)S(1)} collective-permute-done((bf16[1024,128]{1,0:T(8,128)(2,1)S(1)}, bf16[1024,128]{1,0:T(8,128)(2,1)S(1)}, u32[]{:S(2)}, u32[]{:S(2)}) %collective-permute-start.4) | collective-permute-done | bytes 262176 | tf_op jit(solution)/shard_map/ppermute | solution.py:268
  35.6 0.9 %collective-permute-done.5.two = bf16[1024,128]{1,0:T(8,128)(2,1)S(1)} collective-permute-done((bf16[1024,128]{1,0:T(8,128)(2,1)S(1)}, bf16[1024,128]{1,0:T(8,128)(2,1)S(1)}, u32[]{:S(2)}, u32[]{:S(2)}) %collective-permute-start.5) | collective-permute-done | bytes 262176 | tf_op jit(solution)/shard_map/ppermute | solution.py:268
  36.5 0.8 %shard_map.49.refs_0_ = f32[2048,128]{1,0:T(8,128)} custom-call(f32[1024,128]{1,0:T(8,128)S(1)} %get-tuple-element.24.total, bf16[1024,128]{1,0:T(8,128)(2,1)S(1)} %collective-permute-done.4.one, bf16[1024,128]{1,0:T(8,128)(2,1)S(1)} %collective-permute-done.5.two), custom_call_target="tpu_custom_call" | custom-call | flops 1048576 | bytes 2097152 | tf_op jit(solution)/shard_map/pallas_call | solution.py:254
  37.4 3.7 %collective-permute-done.2.one = bf16[1024,128]{1,0:T(8,128)(2,1)S(1)} collective-permute-done((bf16[1024,128]{1,0:T(8,128)(2,1)S(1)}, bf16[1024,128]{1,0:T(8,128)(2,1)S(1)}, u32[]{:S(2)}, u32[]{:S(2)}) %collective-permute-start.2) | collective-permute-done | bytes 262176 | tf_op jit(solution)/shard_map/ppermute | solution.py:268
  41.0 0.0 collective-permute-done.3.two
  41.0 0.8 %shard_map.50 = f32[2048,128]{1,0:T(8,128)} custom-call(f32[1024,128]{1,0:T(8,128)S(1)} %get-tuple-element.21.total, bf16[1024,128]{1,0:T(8,128)(2,1)S(1)} %collective-permute-done.2.one, bf16[1024,128]{1,0:T(8,128)(2,1)S(1)} %collective-permute-done.3.two, f32[2048,128]{1,0:T(8,128)} %shard_map.49.refs_0_), custom_call_target="tpu_custom_call", output_to_operand_aliasing={{}: (3, {})} | custom-call | flops 1048576 | bytes 2097152 | tf_op jit(solution)/shard_map/pallas_call | solution.py:254
Async XLA Ops:
  0.0 21.1 %collective-permute-start.1 = (bf16[2048,128]{1,0:T(8,128)(2,1)}, bf16[2048,128]{1,0:T(8,128)(2,1)S(1)}, u32[]{:S(2)}, u32[]{:S(2)}) collective-permute-start(bf16[2048,128]{1,0:T(8,128)(2,1)} %bitcast.2), channel_id=1, source_target_pairs={{0,1},{1,2},{2,3},{3,4},{4,5},{5,6},{6,7},{7,8},{8,9},{9,10},{10,1... | collective-permute-start | bytes 1572872 | tf_op jit(solution)/shard_map/ppermute | solution.py:268
  1.2 19.9 %collective-permute-start = (bf16[2048,128]{1,0:T(8,128)(2,1)}, bf16[2048,128]{1,0:T(8,128)(2,1)S(1)}, u32[]{:S(2)}, u32[]{:S(2)}) collective-permute-start(bf16[2048,128]{1,0:T(8,128)(2,1)} %bitcast.3), channel_id=1, source_target_pairs={{0,62},{1,63},{2,0},{3,1},{4,2},{5,3},{6,4},{7,5},{8,6},{9,7},{10,... | collective-permute-start | bytes 1572872 | tf_op jit(solution)/shard_map/ppermute | solution.py:268
  9.5 1.6 %copy-start = (f32[4096,128]{1,0:T(8,128)S(1)}, f32[4096,128]{1,0:T(8,128)}, u32[]{:S(2)}) copy-start(f32[4096,128]{1,0:T(8,128)} %constant.8.clone.refs_3_) | copy-start | bytes 6291460
  11.1 1.0 %copy-start.1 = (bf16[1,2048,128]{2,1,0:T(8,128)(2,1)S(1)}, bf16[1,2048,128]{2,1,0:T(8,128)(2,1)}, u32[]{:S(2)}) copy-start(bf16[1,2048,128]{2,1,0:T(8,128)(2,1)} %param.4) | copy-start | bytes 1572868
  12.1 1.0 %copy-start.2 = (bf16[4,256,256]{2,1,0:T(8,128)(2,1)S(1)}, bf16[4,256,256]{2,1,0:T(8,128)(2,1)}, u32[]{:S(2)}) copy-start(bf16[4,256,256]{2,1,0:T(8,128)(2,1)} %constant.6.clone.refs_1_) | copy-start | bytes 1572868
  13.2 0.9 %copy-start.3 = (bf16[4,128,128]{2,1,0:T(8,128)(2,1)S(1)}, bf16[4,128,128]{2,1,0:T(8,128)(2,1)}, u32[]{:S(2)}) copy-start(bf16[4,128,128]{2,1,0:T(8,128)(2,1)} %constant.7.clone.refs_2_) | copy-start | bytes 393220
  24.5 11.1 %collective-permute-start.4 = (bf16[1024,128]{1,0:T(8,128)(2,1)S(1)}, bf16[1024,128]{1,0:T(8,128)(2,1)S(1)}, u32[]{:S(2)}, u32[]{:S(2)}) collective-permute-start(bf16[1024,128]{1,0:T(8,128)(2,1)S(1)} %get-tuple-element.25), channel_id=1, source_target_pairs={{0,2},{1,3},{2,4},{3,5},{4,6},{5,7},{6,8},{7,9},{8,10},{9,11},{10,... | collective-permute-start | bytes 786440 | tf_op jit(solution)/shard_map/ppermute | solution.py:268
  24.6 11.9 %collective-permute-start.5 = (bf16[1024,128]{1,0:T(8,128)(2,1)S(1)}, bf16[1024,128]{1,0:T(8,128)(2,1)S(1)}, u32[]{:S(2)}, u32[]{:S(2)}) collective-permute-start(bf16[1024,128]{1,0:T(8,128)(2,1)S(1)} %get-tuple-element.26), channel_id=1, source_target_pairs={{0,63},{1,0},{2,1},{3,2},{4,3},{5,4},{6,5},{7,6},{8,7},{9,8},{10,9... | collective-permute-start | bytes 786440 | tf_op jit(solution)/shard_map/ppermute | solution.py:268
  30.5 10.5 %collective-permute-start.2 = (bf16[1024,128]{1,0:T(8,128)(2,1)S(1)}, bf16[1024,128]{1,0:T(8,128)(2,1)S(1)}, u32[]{:S(2)}, u32[]{:S(2)}) collective-permute-start(bf16[1024,128]{1,0:T(8,128)(2,1)S(1)} %get-tuple-element.22), channel_id=1, source_target_pairs={{0,2},{1,3},{2,4},{3,5},{4,6},{5,7},{6,8},{7,9},{8,10},{9,11},{10,... | collective-permute-start | bytes 786440 | tf_op jit(solution)/shard_map/ppermute | solution.py:268
  30.6 10.5 %collective-permute-start.3 = (bf16[1024,128]{1,0:T(8,128)(2,1)S(1)}, bf16[1024,128]{1,0:T(8,128)(2,1)S(1)}, u32[]{:S(2)}, u32[]{:S(2)}) collective-permute-start(bf16[1024,128]{1,0:T(8,128)(2,1)S(1)} %get-tuple-element.23), channel_id=1, source_target_pairs={{0,63},{1,0},{2,1},{3,2},{4,3},{5,4},{6,5},{7,6},{8,7},{9,8},{10,9... | collective-permute-start | bytes 786440 | tf_op jit(solution)/shard_map/ppermute | solution.py:268
